TPU v7x, 128 devices: a whole 4x4x4 slice. The times are simulated.
128 devices in a mesh: row: 8 (over x, y_hi), col: 16 (over y_lo, z, core).
Axes of the slice: x: 4, y: 4 (y_hi: 2, y_lo: 2; y = y_hi * 2 + y_lo), z: 4, core: 2. Of those that a mesh axis runs over, the one named last changes fastest.
Arguments:
- feature_grid: bfloat16 [64, 4, 64, 1536], P('row', None, 'col'), may hold values from -40 to 40
- depthwise_kernel: bfloat16 [7, 7, 1536], replicated, may hold values from -0.875 to 0.875
- depthwise_bias: float32 [1536], replicated, may hold values from -3 to 3
- layer_norm_gain: float32 [1536], replicated, may hold values from 0.1 to 1.9
- layer_norm_shift: float32 [1536], replicated, may hold values from -3 to 3
- expansion_weight: bfloat16 [1536, 6144], P(None, 'col'), may hold values from -0.15625 to 0.15625
- expansion_bias: float32 [6144], P('col'), may hold values from -3 to 3
- reduction_weight: bfloat16 [6144, 1536], P('col'), may hold values from -0.078125 to 0.078125
- reduction_bias: float32 [1536], replicated, may hold values from -3 to 3
- layer_branch_scale: float32 [1536], replicated, may hold values from 0.5 to 2
- projector_weight: bfloat16 [1536, 8192], P(None, ('row', 'col')), may hold values from -8 to 8
- projector_bias: bfloat16 [8192], P(('row', 'col')), may hold values from -3 to 3
- input_norm_gain: bfloat16 [8192], P(('row', 'col')), may hold values from 0.099609375 to 1.8984375
- key_value_weight: bfloat16 [8192, 2048], P(('row', 'col')), may hold values from -0.0625 to 0.0625
- key_value_bias: float32 [2048], replicated, may hold values from -3 to 3
- adapter_down_weight: bfloat16 [8192, 128], P(('row', 'col')), may hold values from -0.0625 to 0.0625
- adapter_up_weight: bfloat16 [2, 64, 1024], replicated, may hold values from -0.75 to 0.75
- image_start_positions: int32 [4], replicated, may hold values from 1 to 14336, as said below
- key_value_cotangent: bfloat16 [256, 64, 2048], P(('row', 'col')), may hold values from -0.046875 to 0.046875
Outputs:
- keys_and_values: bfloat16 [256, 64, 2048], P(('row', 'col'))
- down_grad: float32 [8192, 128], P(('row', 'col'))
- up_grad: float32 [2, 64, 1024], replicated
Inputs may be any that keep to these rules, and one draw needn't show every extreme that they name: `image_start_positions`: strictly increasing; text positions stand before each image, so the images' position ranges never meet.
All inputs are finite; a program needn't handle non-finite values.
Results may differ from a plain program's by a relative error of at most 0.022.
Values may be sent and summed in bfloat16 or wider, within the bound.
A program may use at most 192 MiB of HBM per device.

v0:
```python
import math

import jax
import jax.numpy as jnp
from jax import lax
from jax.sharding import PartitionSpec as P

LANGUAGE_WIDTH = 8192
KV_HEADS = 8
HEAD_DIM = 128
ADAPTER_RANK = 64
IMAGES = 4
KEY_VALUE_WIDTH = 1024


adapter_scale = 0.5
rope_theta = 1000000.0


def padded_2(block, sides, width):
    for axis, dim in sides:
        count = lax.axis_size(axis)
        forward = [(i, i + 1) for i in range(count - 1)]
        backward = [(target, source) for source, target in forward]
        low = lax.ppermute(
            lax.slice_in_dim(block, block.shape[dim] - width, None, axis=dim), axis, forward
        )
        high = lax.ppermute(lax.slice_in_dim(block, 0, width, axis=dim), axis, backward)
        block = jnp.concatenate([low, block, high], axis=dim)
    return block


def depth_conv(padded, kernel, bias):
    out_rows = padded.shape[0] - 6
    out_cols = padded.shape[2] - 6
    accum = jnp.zeros((out_rows, padded.shape[1], out_cols, padded.shape[3]), jnp.float32) + bias
    for vertical in range(7):
        for horizontal in range(7):
            window = padded[
                vertical : vertical + out_rows, :, horizontal : horizontal + out_cols, :
            ].astype(jnp.float32)
            accum = accum + window * kernel[vertical, horizontal].astype(jnp.float32)
    return accum


def channel_norm(values, gain, shift):
    center = jnp.mean(values, axis=-1, keepdims=True)
    centered = values - center
    variance = jnp.mean(centered * centered, axis=-1, keepdims=True)
    return centered * lax.rsqrt(variance + 1e-06) * gain + shift


def project_rows(tokens, weight, bias):
    flat_tokens = tokens.reshape(-1, tokens.shape[-1])
    result = jnp.dot(flat_tokens, weight, preferred_element_type=jnp.float32) + bias.astype(
        jnp.float32
    )
    return result.reshape(tokens.shape[:-1] + (weight.shape[1],))


def rms_scale(projected, squares, gain):
    return (
        projected
        * lax.rsqrt(squares[..., None] / LANGUAGE_WIDTH + 1e-06)
        * gain.astype(jnp.float32)
    ).astype(jnp.bfloat16)


def linear_summands(normalized_rows, key_value_weight, adapter_down_weight):
    flattened_normed = normalized_rows.reshape(-1, normalized_rows.shape[-1])
    key_value_summand = jnp.dot(
        flattened_normed, key_value_weight, preferred_element_type=jnp.float32
    )
    adapter_summand = jnp.dot(
        flattened_normed, adapter_down_weight, preferred_element_type=jnp.float32
    )
    leading_dimensions = normalized_rows.shape[:-1]
    return (
        key_value_summand.reshape(leading_dimensions + (key_value_weight.shape[1],)),
        adapter_summand.reshape(leading_dimensions + (adapter_down_weight.shape[1],)),
    )


def rotation(token_positions):
    half_dim = HEAD_DIM // 2
    freq_steps = jnp.arange(half_dim, dtype=jnp.float32)
    inverse = jnp.exp(freq_steps * (-2.0 * math.log(rope_theta) / HEAD_DIM))
    angle = token_positions.astype(jnp.float32)[..., None, None] * inverse
    return (jnp.cos(angle), jnp.sin(angle))


def rotate(values, cosine, sine_part, sign):
    shaped = values.reshape(values.shape[:-1] + (KV_HEADS, HEAD_DIM))
    half_dim = HEAD_DIM // 2
    leading = shaped[..., :half_dim]
    trailing = shaped[..., half_dim:]
    turned = jnp.concatenate(
        [
            leading * cosine - sign * trailing * sine_part,
            trailing * cosine + sign * leading * sine_part,
        ],
        axis=-1,
    )
    return turned.reshape(values.shape)


def finalize(
    key_value_sum,
    adapter_total_sum,
    key_value_bias,
    adapter_up_weight,
    token_positions,
    key_value_cotangent,
):
    seq_count, width_cols = (key_value_sum.shape[0], key_value_sum.shape[1])
    adapter_in = adapter_total_sum.astype(jnp.bfloat16)
    flattened_input = adapter_in.reshape(-1, 2 * ADAPTER_RANK)
    reduced_key = jnp.dot(
        flattened_input[:, :ADAPTER_RANK], adapter_up_weight[0], preferred_element_type=jnp.float32
    )
    reduced_value = jnp.dot(
        flattened_input[:, ADAPTER_RANK:], adapter_up_weight[1], preferred_element_type=jnp.float32
    )
    reduced_rank_part = jnp.concatenate([reduced_key, reduced_value], axis=1).reshape(
        seq_count, width_cols, 2 * KEY_VALUE_WIDTH
    )
    linear_map = key_value_sum + key_value_bias + adapter_scale * reduced_rank_part
    cosine, sine_part = rotation(token_positions)
    rotated_keys = rotate(linear_map[..., :KEY_VALUE_WIDTH], cosine, sine_part, 1.0)
    keys_and_values = jnp.concatenate(
        [rotated_keys, linear_map[..., KEY_VALUE_WIDTH:]], axis=-1
    ).astype(jnp.bfloat16)
    incoming = key_value_cotangent.astype(jnp.float32)
    key_back = rotate(incoming[..., :KEY_VALUE_WIDTH], cosine, sine_part, -1.0)
    linear_grad = jnp.concatenate([key_back, incoming[..., KEY_VALUE_WIDTH:]], axis=-1).astype(
        jnp.bfloat16
    )
    flattened_gradient = linear_grad.reshape(-1, 2 * KEY_VALUE_WIDTH)
    key_gradient = jnp.dot(
        flattened_gradient[:, :KEY_VALUE_WIDTH],
        adapter_up_weight[0].T,
        preferred_element_type=jnp.float32,
    )
    value_gradient = jnp.dot(
        flattened_gradient[:, KEY_VALUE_WIDTH:],
        adapter_up_weight[1].T,
        preferred_element_type=jnp.float32,
    )
    adapter_gradient = (
        adapter_scale * jnp.concatenate([key_gradient, value_gradient], axis=1)
    ).astype(jnp.bfloat16)
    adapter_gradient = adapter_gradient.reshape(seq_count, width_cols, 2 * ADAPTER_RANK)
    key_up_weight = jnp.dot(
        flattened_input[:, :ADAPTER_RANK].T,
        flattened_gradient[:, :KEY_VALUE_WIDTH],
        preferred_element_type=jnp.float32,
    )
    value_up_weight = jnp.dot(
        flattened_input[:, ADAPTER_RANK:].T,
        flattened_gradient[:, KEY_VALUE_WIDTH:],
        preferred_element_type=jnp.float32,
    )
    up_weight_local = adapter_scale * jnp.stack([key_up_weight, value_up_weight])
    return (keys_and_values, adapter_gradient, up_weight_local)


def local(
    feature_grid,
    depthwise_kernel,
    depthwise_bias,
    layer_norm_gain,
    layer_norm_shift,
    expansion_weight,
    expansion_bias,
    reduction_weight,
    reduction_bias,
    layer_branch_scale,
    projector_weight,
    projector_bias,
    input_norm_gain,
    key_value_weight,
    key_value_bias,
    adapter_down_weight,
    adapter_up_weight,
    image_start_positions,
    key_value_cotangent,
):
    tile_rows, image_count, tile_cols, channels = feature_grid.shape
    col_count = lax.axis_size("col")
    col_index = lax.axis_index("col")
    seq_rows = tile_rows * image_count // col_count
    padded = padded_2(feature_grid, (("row", 0), ("col", 2)), 3)
    normed = channel_norm(
        depth_conv(padded, depthwise_kernel, depthwise_bias), layer_norm_gain, layer_norm_shift
    ).astype(jnp.bfloat16)
    hidden = jax.nn.gelu(
        jnp.einsum(
            "hiwc,cf->hiwf",
            lax.all_gather(normed, "col", axis=2, tiled=True),
            expansion_weight,
            preferred_element_type=jnp.float32,
        )
        + expansion_bias,
        approximate=False,
    ).astype(jnp.bfloat16)
    branch_terms = jnp.einsum(
        "hiwf,fc->hiwc", hidden, reduction_weight, preferred_element_type=jnp.float32
    )
    branch_sum = lax.psum_scatter(
        branch_terms.astype(jnp.bfloat16), "col", scatter_dimension=2, tiled=True
    ).astype(jnp.float32)
    encoded_tile = (
        feature_grid.astype(jnp.float32) + layer_branch_scale * (branch_sum + reduction_bias)
    ).astype(jnp.bfloat16)
    ordered = lax.all_to_all(
        encoded_tile.reshape(tile_rows * image_count, tile_cols, channels),
        "col",
        split_axis=0,
        concat_axis=1,
        tiled=True,
    )
    width_cols = ordered.shape[1]
    device_block = lax.axis_index("row") * col_count + col_index
    seq_index = device_block * seq_rows + jnp.arange(seq_rows, dtype=jnp.int32)
    image_match = (seq_index % IMAGES)[:, None] == jnp.arange(IMAGES, dtype=jnp.int32)[None, :]
    offsets = jnp.sum(jnp.where(image_match, image_start_positions[None, :], 0), axis=1)
    token_positions = (offsets + seq_index // IMAGES * width_cols)[:, None] + jnp.arange(
        width_cols, dtype=jnp.int32
    )[None, :]
    gathered = (
        lax.all_gather(projector_weight, "row", axis=1, tiled=True),
        lax.all_gather(projector_bias, "row", axis=0, tiled=True),
        lax.all_gather(input_norm_gain, "row", axis=0, tiled=True),
        lax.all_gather(key_value_weight, "row", axis=0, tiled=True),
        lax.all_gather(adapter_down_weight, "row", axis=0, tiled=True),
    )
    proj_local, bias_local, gain_local, kv_local, down_local = gathered
    projected = project_rows(
        lax.all_gather(ordered, "col", axis=0, tiled=True), proj_local, bias_local
    )
    squares = lax.psum(jnp.sum(projected * projected, axis=-1), "col")
    normalized_rows = rms_scale(projected, squares, gain_local)
    key_value_summand, adapter_summand = linear_summands(normalized_rows, kv_local, down_local)
    key_value_sum, adapter_total_sum = (
        lax.psum_scatter(
            key_value_summand.astype(jnp.bfloat16), "col", scatter_dimension=0, tiled=True
        ).astype(jnp.float32),
        lax.psum_scatter(
            adapter_summand.astype(jnp.bfloat16), "col", scatter_dimension=0, tiled=True
        ).astype(jnp.float32),
    )
    keys_and_values, adapter_gradient, up_weight_local = finalize(
        key_value_sum,
        adapter_total_sum,
        key_value_bias,
        adapter_up_weight,
        token_positions,
        key_value_cotangent,
    )
    down_part = jnp.einsum(
        "rwd,rwk->dk",
        normalized_rows,
        lax.all_gather(adapter_gradient, "col", axis=0, tiled=True),
        preferred_element_type=jnp.float32,
    )
    down_grad = lax.psum_scatter(
        down_part.astype(jnp.bfloat16), "row", scatter_dimension=0, tiled=True
    ).astype(jnp.float32)
    up_grad = lax.psum(up_weight_local, ("row", "col"))
    return (keys_and_values, down_grad, up_grad)


def solution(mesh):
    in_specs = (
        P("row", None, "col", None),
        P(),
        P(),
        P(),
        P(),
        P(None, "col"),
        P("col"),
        P("col", None),
        P(),
        P(),
        P(None, ("row", "col")),
        P(("row", "col")),
        P(("row", "col")),
        P(("row", "col"), None),
        P(),
        P(("row", "col"), None),
        P(),
        P(),
        P(("row", "col"), None, None),
    )
    out_specs = (P(("row", "col"), None, None), P(("row", "col"), None), P())
    return jax.shard_map(local, mesh=mesh, in_specs=in_specs, out_specs=out_specs, check_vma=False)
```

profile of v0, /device:TPU:1, one launch (start us, length us, event | category | flops | bytes accessed | tf_op | source)
XLA Modules:
  0.0 665.5 jit_solution(14815263644281419149)
XLA Ops:
  8.1 1.3 constant_dynamic-update-slice_fusion.1
  9.5 5.8 collective-permute-start
  15.3 1.3 collective-permute-start.1
  16.6 2.2 collective-permute-done
  18.9 5.3 collective-permute-done.1
  24.2 0.4 pad_maximum_fusion.1
  24.7 0.4 copy.66
  25.1 5.3 collective-permute-start.2
  30.4 0.4 copy.69
  30.8 1.9 collective-permute-start.3
  32.8 0.2 convert_reduce_fusion.46
  33.0 0.3 convert_reduce_fusion.48
  33.3 0.3 convert_reduce_fusion.47
  33.7 2.7 collective-permute-done.2
  36.5 4.7 collective-permute-done.3
  41.3 1.1 maximum_maximum_fusion
  42.5 8.5 %fusion.137 = (f32[8,4,4]{0,2,1:T(4,128)S(1)}, f32[8,4,4,1536]{3,0,2,1:T(8,128)S(1)}) fusion(f32[1536]{0:T(1024)S(1)} %get-tuple-element.52, bf16[14,4,7,1536]{3,0,2,1:T(8,128)(2,1)S(1)} %get-tuple-element.59, f32[1536]{0:T(1024)S(1)} %get-tuple-element.53, f32[1536]{0:T(1024)S(1)} %get-tuple-element.6, f32[1536]{0:T(1024)S(1)} %get-tuple-element.7, ...), kind=kLoop, calls=%fused_computation.250 | loop fusion | flops 30867328 | bytes 19329536 | tf_op jit(solution)/shard_map/reduce_sum | solution.py:47
  50.9 0.2 multiply_reduce_fusion.1
  51.2 0.2 add_convert_fusion
  51.4 0.8 copy.72
  52.2 0.2 reduce-scatter.5.cloned.1.call-start
  52.4 44.3 %all-gather.5.cloned.1.call-done = bf16[8,4,64,1536]{3,0,1,2:T(8,128)(2,1)} async-done(((bf16[8,4,4,1536]{3,0,1,2:T(8,128)(2,1)}), bf16[8,4,64,1536]{3,0,1,2:T(8,128)(2,1)}) %all-gather.5.cloned.1.call-update) | async-done | bytes 6291472 | tf_op jit(solution)/shard_map/all_gather | solution.py:199
  96.7 11.5 %fusion.79 = (u8[4,64,384]{2,1,0:T(8,128)(4,1)S(1)}, u8[4,64,384]{2,1,0:T(8,128)(4,1)S(1)}, f32[8,4,64,384]{3,2,1,0:T(8,128)S(1)}) fusion(f32[384]{0:T(512)S(1)} %copy-done.16, bf16[1536,384]{1,0:T(8,128)(2,1)S(1)} %copy-done.15, bf16[8,4,64,1536]{3,0,1,2:T(8,128)(2,1)} %all-gather.5.cloned.1.call-done), kind=kOutput, calls=%fused_computation.113 | convolution fusion | flops 2426732544 | bytes 10814976 | tf_op jit(solution)/shard_map/hiwc,cf->hiwf/dot_general | solution.py:197
  108.3 10.2 %convolution_convert_fusion.1 = bf16[8,4,64,1536]{3,2,1,0:T(8,128)(2,1)S(1)} fusion(f32[8,4,64,384]{3,2,1,0:T(8,128)S(1)} %get-tuple-element.77, f32[384]{0:T(512)S(1)} %copy-done.16, bf16[384,1536]{1,0:T(8,128)(2,1)S(1)} %copy-done, u8[4,64,384]{2,1,0:T(8,128)(4,1)S(1)} %get-tuple-element.4, u8[4,64,384]{2,1,0:T(8,128)(4,1)S(1)} %get-tuple-element.3), kind=kOutput, calls=%fused_computation.3 | convolution fusion | flops 2474901504 | bytes 10814976 | tf_op jit(solution)/shard_map/hiwf,fc->hiwc/dot_general | solution.py:206
  118.5 6.2 copy.74
  124.8 0.5 all-gather.9.cloned.1.call-update
  125.4 75.8 %reduce-scatter.5.cloned.1.call-done = bf16[8,4,4,1536]{3,0,1,2:T(8,128)(2,1)} async-done(((bf16[8,4,64,1536]{3,0,1,2:T(8,128)(2,1)}), bf16[8,4,4,1536]{3,0,1,2:T(8,128)(2,1)}) %reduce-scatter.5.cloned.1.call-update) | async-done | bytes 393232 | tf_op jit(solution)/shard_map/reduce_scatter | solution.py:209
  201.2 1.2 fusion.77
  202.4 0.2 copy.76
  202.6 15.8 %all_to_all.18 = bf16[32,4,1536]{2,1,0:T(4,128)(2,1)S(1)} all-to-all(bf16[32,4,1536]{2,1,0:T(4,128)(2,1)S(1)} %bitcast.83), channel_id=1, replica_groups=mesh['row'=8,'col'=16] {'col'}, dimensions={0} | all-to-all | bytes 786432 | tf_op jit(solution)/shard_map/all_to_all | solution.py:215
  218.4 0.3 copy.77
  218.7 0.8 copy.78
  219.6 0.5 all-gather.11.cloned.1.call-update
  220.2 0.6 dynamic-slice
  221.5 0.2 dynamic-update-slice
  221.7 0.2 dynamic-update-slice.1
  222.0 21.0 %all-reduce.2 = (bf16[512]{0:T(512)(128)(2,1)S(1)}, bf16[512]{0:T(512)(128)(2,1)S(1)}) all-reduce(bf16[512]{0:T(512)(128)(2,1)S(1)} %dynamic-update-slice, bf16[512]{0:T(512)(128)(2,1)S(1)} %dynamic-update-slice.1), channel_id=1, replica_groups=mesh['row'=8,'col'=16] {'row'}, use_global_device_ids=true, to_apply=%add | all-reduce | flops 1024 | bytes 4096
  243.0 28.5 %all_gather.30 = bf16[512,128]{1,0:T(8,128)(2,1)S(1)} all-gather(bf16[64,128]{1,0:T(8,128)(2,1)S(1)} %copy-done.8), channel_id=1, replica_groups=mesh['row'=8,'col'=16] {'row'}, dimensions={0}, use_global_device_ids=true | all-gather | bytes 147456 | tf_op jit(solution)/shard_map/all_gather | solution.py:235
  271.5 8.7 %multiply_reduce_fusion = (f32[2048]{0:T(1024)S(1)}, f32[2048,512]{1,0:T(8,128)}) fusion(f32[512]{0:T(512)S(1)} %convert_element_type.849, bf16[2048,1536]{1,0:T(8,128)(2,1)} %bitcast.91, bf16[1536,512]{0,1:T(8,128)(2,1)} %all-gather.9.cloned.1.call-done), kind=kOutput, calls=%fused_computation.7 | convolution fusion | flops 3224369152 | bytes 12068864 | tf_op jit(solution)/shard_map/dot_general | solution.py:55
  280.3 59.5 %psum.14 = f32[32,64]{1,0:T(8,128)S(1)} all-reduce(f32[32,64]{1,0:T(8,128)S(1)} %reduce_sum.41), channel_id=1, replica_groups=mesh['row'=8,'col'=16] {'col'}, use_global_device_ids=true, to_apply=%region_4.5 | all-reduce | flops 2048 | bytes 16384 | tf_op jit(solution)/shard_map/psum | solution.py:241
  339.9 2.6 multiply_convert_fusion.1
  342.5 1.5 convolution_convert_fusion.2
  344.1 8.3 %convolution_convert_fusion = bf16[32,64,2048]{2,1,0:T(8,128)(2,1)} fusion(bf16[32,64,512]{2,1,0:T(8,128)(2,1)S(1)} %bitcast.76, bf16[512,2048]{1,0:T(8,128)(2,1)} %all-gather.11.cloned.1.call-done), kind=kOutput, calls=%fused_computation.2 | convolution fusion | flops 4299161600 | bytes 12582912 | tf_op jit(solution)/shard_map/dot_general | solution.py:71
  352.5 1.0 copy-done.6
  354.0 0.3 broadcast_multiply_fusion
  354.3 0.2 fusion.86
  354.5 44.6 %reduce-scatter.9.cloned.1.call-done = bf16[2,64,128]{2,1,0:T(8,128)(2,1)} async-done(((bf16[32,64,128]{2,1,0:T(8,128)(2,1)}), bf16[2,64,128]{2,1,0:T(8,128)(2,1)}) %reduce-scatter.9.cloned.1.call-update) | async-done | bytes 32784 | tf_op jit(solution)/shard_map/reduce_scatter | solution.py:248
  399.1 1.0 fusion.90
  400.1 1.0 fusion.92
  401.2 73.6 %reduce-scatter.7.cloned.1.call-done = bf16[2,64,2048]{2,1,0:T(8,128)(2,1)} async-done(((bf16[32,64,2048]{2,1,0:T(8,128)(2,1)}), bf16[2,64,2048]{2,1,0:T(8,128)(2,1)}) %reduce-scatter.7.cloned.1.call-update) | async-done | bytes 524304 | tf_op jit(solution)/shard_map/reduce_scatter | solution.py:245
  474.7 1.2 add_add_fusion
  476.0 0.5 subtract_convert_fusion
  476.5 1.0 pad_maximum_fusion.4
  477.6 1.1 fusion.88
  478.8 22.1 %all_gather.31 = bf16[32,64,128]{2,1,0:T(8,128)(2,1)S(1)} all-gather(bf16[2,64,128]{2,1,0:T(8,128)(2,1)S(1)} %fusion.99), channel_id=1, replica_groups=mesh['row'=8,'col'=16] {'col'}, dimensions={0}, use_global_device_ids=true | all-gather | bytes 557056 | tf_op jit(solution)/shard_map/all_gather | solution.py:263
  500.9 4.1 fusion.51
  505.1 0.3 convolution_bitcast_fusion
  505.4 0.2 convolution_bitcast_fusion.1
  505.6 0.8 maximum_multiply_fusion.1
  506.6 0.8 pad_maximum_fusion.2
  507.5 64.5 %reduce-scatter.11.cloned.1.call-done = bf16[64,128]{1,0:T(8,128)(2,1)} async-done(((bf16[512,128]{1,0:T(8,128)(2,1)}), bf16[64,128]{1,0:T(8,128)(2,1)}) %reduce-scatter.11.cloned.1.call-update) | async-done | bytes 16400 | tf_op jit(solution)/shard_map/reduce_scatter | solution.py:266
  572.0 1.3 convert_element_type.859
  573.3 83.2 %all-reduce.5.cloned.1.call-done = f32[2,64,1024]{2,1,0:T(8,128)} async-done(((f32[2,64,1024]{2,1,0:T(8,128)}), f32[2,64,1024]{2,1,0:T(8,128)}) %all-reduce.5.cloned.1.call-update) | async-done | bytes 524304 | tf_op jit(solution)/shard_map/psum | solution.py:269
  656.5 1.9 copy.100
  (87 shorter events, 2.4 us)
Async XLA Ops:
  8.0 100.3 %copy-start = (bf16[384,1536]{1,0:T(8,128)(2,1)S(1)}, bf16[384,1536]{1,0:T(8,128)(2,1)}, u32[]{:S(2)}) copy-start(bf16[384,1536]{1,0:T(8,128)(2,1)} %param.26) | copy-start | bytes 3538948
  8.0 88.7 %all-gather.5.cloned.1.call-start = ((), (), s32[]{:S(2)}) async-start(), calls=%async_computation.5 | async-start | bytes 6684672 | tf_op jit(solution)/shard_map/all_gather | solution.py:199
  9.5 23.2 %copy-start.5 = (bf16[7,7,1536]{2,1,0:T(8,128)(2,1)S(1)}, bf16[7,7,1536]{2,1,0:T(8,128)(2,1)}, u32[]{:S(2)}) copy-start(bf16[7,7,1536]{2,1,0:T(8,128)(2,1)} %param.20) | copy-start | bytes 451588
  9.5 9.3 %collective-permute-start = (bf16[3,4,4,1536]{3,0,2,1:T(4,128)(2,1)S(1)}, bf16[3,4,4,1536]{3,0,2,1:T(4,128)(2,1)S(1)}, u32[]{:S(2)}, u32[]{:S(2)}) collective-permute-start(bf16[3,4,4,1536]{3,0,2,1:T(4,128)(2,1)S(1)} %get-tuple-element.70), channel_id=1, source_target_pairs={{0,16},{16,32},{32,48},{48,64},{64,80},{80,96},{96,112},{1,17},{17... | collective-permute-start | bytes 442376 | tf_op jit(solution)/shard_map/ppermute | solution.py:25
  15.3 8.8 %collective-permute-start.1 = (bf16[3,4,4,1536]{3,0,2,1:T(4,128)(2,1)S(1)}, bf16[3,4,4,1536]{3,0,2,1:T(4,128)(2,1)S(1)}, u32[]{:S(2)}, u32[]{:S(2)}) collective-permute-start(bf16[3,4,4,1536]{3,0,2,1:T(4,128)(2,1)S(1)} %get-tuple-element.71), channel_id=1, source_target_pairs={{16,0},{32,16},{48,32},{64,48},{80,64},{96,80},{112,96},{17,1},{33... | collective-permute-start | bytes 442376 | tf_op jit(solution)/shard_map/ppermute | solution.py:28
  25.1 11.3 %collective-permute-start.2 = (bf16[14,4,3,1536]{3,1,2,0:T(4,128)(2,1)S(1)}, bf16[14,4,3,1536]{3,1,2,0:T(4,128)(2,1)S(1)}, u32[]{:S(2)}, u32[]{:S(2)}) collective-permute-start(bf16[14,4,3,1536]{3,1,2,0:T(4,128)(2,1)S(1)} %copy.66), channel_id=1, source_target_pairs={{0,1},{1,2},{2,3},{3,4},{4,5},{5,6},{6,7},{7,8},{8,9},{9,10},{10,1... | collective-permute-start | bytes 1548296 | tf_op jit(solution)/shard_map/ppermute | solution.py:25
  30.8 10.4 %collective-permute-start.3 = (bf16[14,4,3,1536]{3,1,2,0:T(4,128)(2,1)S(1)}, bf16[14,4,3,1536]{3,1,2,0:T(4,128)(2,1)S(1)}, u32[]{:S(2)}, u32[]{:S(2)}) collective-permute-start(bf16[14,4,3,1536]{3,1,2,0:T(4,128)(2,1)S(1)} %copy.69), channel_id=1, source_target_pairs={{1,0},{2,1},{3,2},{4,3},{5,4},{6,5},{7,6},{8,7},{9,8},{10,9},{11,1... | collective-permute-start | bytes 1548296 | tf_op jit(solution)/shard_map/ppermute | solution.py:28
  36.5 5.9 copy-start.9
  42.4 8.7 %copy-start.10 = (f32[1536]{0:T(1024)S(1)}, f32[1536]{0:T(1024)}, u32[]{:S(2)}) copy-start(f32[1536]{0:T(1024)} %param.23) | copy-start | bytes 18436
  42.4 8.7 %copy-start.11 = (f32[1536]{0:T(1024)S(1)}, f32[1536]{0:T(1024)}, u32[]{:S(2)}) copy-start(f32[1536]{0:T(1024)} %param.22) | copy-start | bytes 18436
  50.9 45.8 %copy-start.15 = (bf16[1536,384]{1,0:T(8,128)(2,1)S(1)}, bf16[1536,384]{1,0:T(8,128)(2,1)}, u32[]{:S(2)}) copy-start(bf16[1536,384]{1,0:T(8,128)(2,1)} %param.24) | copy-start | bytes 3538948
  50.9 45.8 %copy-start.16 = (f32[384]{0:T(512)S(1)}, f32[384]{0:T(512)}, u32[]{:S(2)}) copy-start(f32[384]{0:T(512)} %param.25) | copy-start | bytes 4612
  52.2 149.0 %reduce-scatter.5.cloned.1.call-start = ((), (), s32[]{:S(2)}) async-start(), calls=%async_computation.6 | async-start | bytes 6684672 | tf_op jit(solution)/shard_map/reduce_scatter | solution.py:209
  124.7 76.5 %copy-start.2 = (bf16[8,4,4,1536]{3,2,1,0:T(4,128)(2,1)S(1)}, bf16[8,4,4,1536]{3,2,1,0:T(4,128)(2,1)}, u32[]{:S(2)}) copy-start(bf16[8,4,4,1536]{3,2,1,0:T(4,128)(2,1)} %param.19) | copy-start | bytes 1179652
  124.7 76.5 %copy-start.12 = (f32[1536]{0:T(1024)S(1)}, f32[1536]{0:T(1024)}, u32[]{:S(2)}) copy-start(f32[1536]{0:T(1024)} %param.27) | copy-start | bytes 18436
  124.7 76.5 %copy-start.13 = (f32[1536]{0:T(1024)S(1)}, f32[1536]{0:T(1024)}, u32[]{:S(2)}) copy-start(f32[1536]{0:T(1024)} %param.28) | copy-start | bytes 18436
  124.7 95.5 %copy-start.20 = (u32[128]{0:T(128)S(1)}, u32[128]{0:T(128)}, u32[]{:S(2)}) copy-start(u32[128]{0:T(128)} %constant.130) | copy-start | bytes 1540
  124.7 96.7 %copy-start.17 = (bf16[64]{0:T(256)(128)(2,1)S(1)}, bf16[64]{0:T(256)(128)(2,1)}, u32[]{:S(2)}) copy-start(bf16[64]{0:T(256)(128)(2,1)} %param.30) | copy-start | bytes 388
  124.7 97.0 %copy-start.18 = (bf16[64]{0:T(256)(128)(2,1)S(1)}, bf16[64]{0:T(256)(128)(2,1)}, u32[]{:S(2)}) copy-start(bf16[64]{0:T(256)(128)(2,1)} %param.31) | copy-start | bytes 388
  124.8 118.2 %copy-start.8 = (bf16[64,128]{1,0:T(8,128)(2,1)S(1)}, bf16[64,128]{1,0:T(8,128)(2,1)}, u32[]{:S(2)}) copy-start(bf16[64,128]{1,0:T(8,128)(2,1)} %param.34) | copy-start | bytes 49156
  124.8 146.7 %all-gather.9.cloned.1.call-start = ((), (), s32[]{:S(2)}) async-start(), calls=%async_computation.8 | async-start | bytes 1769472 | tf_op jit(solution)/shard_map/all_gather | solution.py:231
  125.3 146.1 %all-gather.7.cloned.1.call-start = ((), (), s32[]{:S(2)}) async-start(), calls=%async_computation.7 | async-start | bytes 6684672 | tf_op jit(solution)/shard_map/all_gather | solution.py:239
  219.6 124.6 %all-gather.11.cloned.1.call-start = ((), (), s32[]{:S(2)}) async-start(), calls=%async_computation.9 | async-start | bytes 2359296 | tf_op jit(solution)/shard_map/all_gather | solution.py:234
  220.1 178.9 %reduce-scatter.9.cloned.1.call-start = ((), (), s32[]{:S(2)}) async-start(), calls=%async_computation.11 | async-start | bytes 557056 | tf_op jit(solution)/shard_map/reduce_scatter | solution.py:248
  344.1 130.6 %reduce-scatter.7.cloned.1.call-start = ((), (), s32[]{:S(2)}) async-start(), calls=%async_computation.10 | async-start | bytes 8912896 | tf_op jit(solution)/shard_map/reduce_scatter | solution.py:245
  352.4 1.0 copy-start.6
  352.4 1.3 copy-start.19
  352.4 1.9 copy-start.4
  352.4 219.6 %reduce-scatter.11.cloned.1.call-start = ((), (), s32[]{:S(2)}) async-start(), calls=%async_computation.12 | async-start | bytes 147456 | tf_op jit(solution)/shard_map/reduce_scatter | solution.py:266
  353.4 121.3 %copy-start.14 = (f32[2048]{0:T(1024)S(1)}, f32[2048]{0:T(1024)}, u32[]{:S(2)}) copy-start(f32[2048]{0:T(1024)} %param.33) | copy-start | bytes 24580
  477.6 27.5 %copy-start.7 = (bf16[2,64,128]{2,1,0:T(8,128)(2,1)S(1)}, bf16[2,64,128]{2,1,0:T(8,128)(2,1)}, u32[]{:S(2)}) copy-start(bf16[2,64,128]{2,1,0:T(8,128)(2,1)} %reduce-scatter.9.cloned.1.call-done) | copy-start | bytes 98308
  500.9 5.6 copy-start.3
  500.9 157.5 %copy-start.1 = (bf16[384,1536]{1,0:T(8,128)(2,1)S(1)}, bf16[384,1536]{1,0:T(8,128)(2,1)}, u32[]{:S(2)}) copy-start(bf16[384,1536]{1,0:T(8,128)(2,1)} %param.26) | copy-start | bytes 3538948
  505.1 151.4 %all-reduce.5.cloned.1.call-start = ((), (), s32[]{:S(2)}) async-start(), calls=%async_computation.13 | async-start | bytes 1048576 | tf_op jit(solution)/shard_map/psum | solution.py:269
Sparse Core Ops, SparseCore 0:
  52.3 44.3 all-gather.4
  124.8 76.2 reduce-scatter.4
  512.0 144.5 all-reduce.4
Sparse Core Ops, SparseCore 1:
  127.6 50.4 all-gather.8
  219.6 44.3 all-gather.6
  266.2 54.4 all-gather.10
  344.2 54.9 reduce-scatter.8
  401.6 73.0 reduce-scatter.6
  505.1 66.8 reduce-scatter.10
where the time goes:
time: 666 us
  waiting for transfers between devices  402 us (60%)
  blocking collectives  147 us (22%)
  matrix products  48.1 us (7%)
  other arithmetic  21.5 us (3%)
  between operations  16.5 us (2%)
  local copies, waits for them, and re-layouts  15.6 us (2%)
  starting transfers between devices  14.9 us (2%)
    psum x1, waiting for transfers between devices, local(): up_grad = lax.psum(up_weight_local, ('row', 'col'))  83.2 us
    reduce_scatter x1, waiting for transfers between devices, local(): lax.psum_scatter(branch_terms.astype(jnp.bfloat16), 'col', scatter_dimens...  75.8 us
    reduce_scatter x1, waiting for transfers between devices, local(): lax.psum_scatter(key_value_summand.astype(jnp.bfloat16), 'col', scatter_d...  73.6 us
    reduce_scatter x1, waiting for transfers between devices, local(): lax.psum_scatter(down_part.astype(jnp.bfloat16), 'row', scatter_dimension...  64.5 us
    psum x1, blocking collectives, local(): squares = lax.psum(jnp.sum(projected * projected, axis=-1), 'col')  59.5 us
    reduce_scatter x1, waiting for transfers between devices, local(): lax.psum_scatter(adapter_summand.astype(jnp.bfloat16), 'col', scatter_dim...  44.6 us
    all_gather x1, waiting for transfers between devices, local(): lax.all_gather(normed, 'col', axis=2, tiled=True)  44.3 us
    all_gather x1, blocking collectives, local(): lax.all_gather(adapter_down_weight, 'row', axis=0, tiled=True)  28.5 us
  transfers between devices with their start and end apart: 13, of which 10 were waited for; matrix products, arithmetic and copies ran while one was open for 5% of the time, Pallas kernels for 0%

commit v1 on v0

v1 whole, which is shorter than its diff:
```python
import functools
import math

import jax
import jax.numpy as jnp
from jax import lax
from jax.experimental import pallas as pl
from jax.experimental.pallas import tpu as pltpu
from jax.sharding import PartitionSpec as P

LANGUAGE_WIDTH = 8192
HEAD_DIM = 128
IMAGES = 4
CHANNELS = 1536
BLOCKS = 12
EXT = 1664
ROPE_THETA = 1000000.0
MESH = pl.DeviceIdType.MESH
BF = jnp.bfloat16
F32 = jnp.float32
COPIES = 160
SLOT_OF = {0: 0, 3: 1, 1: 2, 2: 3}
OFFSET = (0, -1, 1, 2)


def dot(a, b):
    return jnp.dot(a, b, preferred_element_type=F32)


def dot_tn(a, b):
    return lax.dot_general(a, b, (((0,), (0,)), ((), ())), preferred_element_type=F32)


def dot_nt(a, b):
    return lax.dot_general(a, b, (((1,), (1,)), ((), ())), preferred_element_type=F32)


def kernel(
    x_ref, taps_ref, vec_ref, w1_ref, w2_ref, b1_ref, pt_ref, gb_ref, gain_ref,
    up_ref, cos_ref, sin_ref, cot_ref, kvb_ref, perm_ref, seq_ref,
    kv_ref, down_ref, upg_ref,
    pad, conv, tok, wa, wb, ba, feat, acc, part, rs_in, stage_t, stage_b, seq_in,
    pb, quad, red_in, red_bias, mf, ext, lin, grad,
    ein, e_in1, e_in2, e_all, send, recv, lsem,
):
    row = lax.axis_index("row")
    col = lax.axis_index("col")
    x = row // 2
    y = (row % 2) * 2 + col // 8
    z = (col % 8) // 2
    core = col % 2
    ylo = y % 2
    plane = y * 4 + z
    pair = x * 2 + core

    def device(dx, dy, dz, dk):
        xx, yy, zz, kk = (x + dx + 4) % 4, (y + dy + 4) % 4, (z + dz + 4) % 4, (core + dk) % 2
        return (xx * 2 + yy // 2, (yy % 2) * 8 + zz * 2 + kk)

    ids = [0]

    def push(src, dst, target):
        n = ids[0]
        ids[0] += 1
        copy = pltpu.make_async_remote_copy(
            src_ref=src, dst_ref=dst, send_sem=send.at[n], recv_sem=recv.at[n],
            device_id=target, device_id_type=MESH,
        )
        copy.start()
        return copy

    planes = [(dy, dz) for dy in range(4) for dz in range(4) if (dy, dz) != (0, 0)]
    up_dev = ((row + 7) % 8, col)
    dn_dev = ((row + 1) % 8, col)
    lt_dev = (row, (col + 15) % 16)
    rt_dev = (row, (col + 1) % 16)
    other = device(0, 0, 0, 1)
    yflip = 1 - 2 * ylo

    partners = [up_dev, dn_dev, lt_dev, rt_dev]
    for dx in range(4):
        for dk in range(2):
            if (dx, dk) != (0, 0):
                partners.append(device(dx, 0, 0, dk))
    for dy, dz in planes:
        partners.append(device(0, dy, dz, 0))
    partners.append(device(0, yflip, 0, 1))
    barrier = pltpu.get_barrier_semaphore()
    for partner in partners:
        pl.semaphore_signal(barrier, inc=1, device_id=partner, device_id_type=MESH)
    copies0 = [
        pltpu.make_async_copy(x_ref, pad.at[3:7, 16:48], lsem.at[0]),
        pltpu.make_async_copy(w1_ref, wa.at[0], lsem.at[1]),
        pltpu.make_async_copy(w2_ref, wb.at[0], lsem.at[2]),
        pltpu.make_async_copy(b1_ref, ba.at[0], lsem.at[3]),
        pltpu.make_async_copy(pt_ref, pb.at[0, :, 0:EXT], lsem.at[4]),
        pltpu.make_async_copy(gb_ref.at[pair], pb.at[0, :, EXT:2048], lsem.at[5]),
    ]
    for copy in copies0:
        copy.start()
    pl.semaphore_wait(barrier, len(partners))

    h_up = push(x_ref.at[:, 0:16], pad.at[3:7, 48:64], up_dev)
    h_dn = push(x_ref.at[:, 16:32], pad.at[3:7, 0:16], dn_dev)
    h_rt = push(x_ref.at[1:4], pad.at[0:3, 16:48], rt_dev)
    h_lt = push(x_ref.at[0:3], pad.at[7:10, 16:48], lt_dev)
    gb_copies = []
    pt_copies = []
    for dx in (1, 3, 2):
        pt_copies.append(push(pt_ref, pb.at[2 * dx, :, 0:EXT], device(dx, 0, 0, 0)))
    for dx in range(4):
        for dk in range(2):
            if (dx, dk) != (0, 0):
                target_pair = ((x + dx) % 4) * 2 + (core + dk) % 2
                gb_copies.append(
                    push(gb_ref.at[target_pair], pb.at[2 * dx + dk, :, EXT:2048], device(dx, 0, 0, dk))
                )
    fwd_copies = [push(pt_ref, pb.at[1, :, 0:EXT], other)]
    w_core = [
        push(w1_ref, wa.at[1], other), push(w2_ref, wb.at[1], other), push(b1_ref, ba.at[1], other),
    ]
    w_y = [
        push(w1_ref, wa.at[2], device(0, 1, 0, 0)),
        push(w2_ref, wb.at[2], device(0, 3, 0, 0)),
        push(b1_ref, ba.at[2], device(0, 1, 0, 0)),
    ]

    cosine = cos_ref[...]
    sine = sin_ref[...]
    for head in range(8):
        lanes = slice(head * 128, head * 128 + 128)
        value = cot_ref[:, lanes].astype(F32)
        grad[:, lanes] = (value * cosine - pltpu.roll(value, 64, 1) * sine).astype(BF)
    grad[:, 1024:2048] = cot_ref[:, 1024:2048]
    adapter_grad = dot_nt(grad[...], up_ref[...]).astype(BF).astype(F32)
    for copy in copies0:
        copy.wait()
    for n in range(3):
        lanes = slice(n * 512, n * 512 + 512)
        feat[:, lanes] = dot(perm_ref[...], x_ref[:, :, lanes].reshape(128, 512))

    h_up.wait()
    h_dn.wait()

    @pl.when(row == 0)
    def _():
        pad[3:7, 0:16] = jnp.zeros((4, 16, CHANNELS), BF)

    @pl.when(row == 7)
    def _():
        pad[3:7, 48:64] = jnp.zeros((4, 16, CHANNELS), BF)

    corners = [
        push(pad.at[4:7, 0:16], pad.at[0:3, 0:16], rt_dev),
        push(pad.at[4:7, 48:64], pad.at[0:3, 48:64], rt_dev),
        push(pad.at[3:6, 0:16], pad.at[7:10, 0:16], lt_dev),
        push(pad.at[3:6, 48:64], pad.at[7:10, 48:64], lt_dev),
    ]

    for n, dx in enumerate((1, 3, 2)):
        pt_copies[n].wait()
        fwd_copies.append(push(pb.at[2 * dx, :, 0:EXT], pb.at[2 * dx + 1, :, 0:EXT], other))
    for copy in gb_copies:
        copy.wait()
    for copy in fwd_copies:
        copy.wait()

    def products(i, carry):
        left = pb[:, :, pl.ds(pl.multiple_of(i * 128, 128), 128)].reshape(512, 128)
        for t in range(3):
            block = pair * 3 + t
            shift = i + block - 17
            around = jnp.where(shift >= 13, shift - 13, shift)
            start = jnp.where(block < 17, 13 + t, around) * 128
            right = pb[:, :, pl.ds(pl.multiple_of(start, 128), 128)].reshape(512, 128)
            value = dot_tn(left, right).astype(BF)
            quad[pl.ds(i * 8, 8), :, t * 128:t * 128 + 128] = value.reshape(8, 16, 128)
        return carry

    lax.fori_loop(0, 13, products, 0)
    red_copies = []
    for n, (dy, dz) in enumerate(planes):
        target_plane = ((y + dy) % 4) * 4 + (z + dz) % 4
        target = device(0, dy, dz, 0)
        red_copies.append(push(quad.at[pl.ds(target_plane * 6, 6)], red_in.at[n], target))
        red_copies.append(push(quad.at[96:97], red_bias.at[n], target))

    h_rt.wait()
    h_lt.wait()
    for copy in corners:
        copy.wait()

    @pl.when(col == 0)
    def _():
        pad[0:3] = jnp.zeros((3, 64, CHANNELS), BF)

    @pl.when(col == 15)
    def _():
        pad[7:10] = jnp.zeros((3, 64, CHANNELS), BF)

    def conv_lanes(n, carry):
        lanes = pl.ds(pl.multiple_of(n * 128, 128), 128)
        sums = [jnp.zeros((32, 128), F32) + vec_ref[0:1, lanes] for _ in range(4)]
        for wp in range(10):
            full = pad[wp, :, lanes].astype(F32)
            moved = pltpu.roll(full, 60, 0)
            for a in range(7):
                start = 4 * (a + 1)
                window = full[start:start + 32] if a % 2 else moved[start - 4:start + 28]
                for w in range(max(0, wp - 6), min(3, wp) + 1):
                    tap = a * 7 + wp - w
                    sums[w] = sums[w] + window * taps_ref[tap:tap + 1, lanes]
        for w in range(4):
            conv[w, :, lanes] = sums[w]
        return carry

    lax.fori_loop(0, BLOCKS, conv_lanes, 0)

    def norm_rows(n, carry):
        w = n // 2
        rows = pl.ds(pl.multiple_of((n % 2) * 16, 16), 16)
        value = conv[w, rows, :]
        center = jnp.sum(value, axis=-1, keepdims=True) * (1.0 / CHANNELS)
        centered = value - center
        variance = jnp.sum(centered * centered, axis=-1, keepdims=True) * (1.0 / CHANNELS)
        value = centered * lax.rsqrt(variance + 1e-06) * vec_ref[1:2, :] + vec_ref[2:3, :]
        part[0, w, rows, :] = value.astype(BF)
        return carry

    lax.fori_loop(0, 8, norm_rows, 0)
    for n in range(3):
        lanes = slice(n * 512, n * 512 + 512)
        tok[0, :, lanes] = dot(perm_ref[...], part[0, :, :, lanes].reshape(128, 512)).astype(BF)
    t_next = push(tok.at[0], tok.at[1], device(0, 0, 1, 0))
    t_prev = push(tok.at[0], tok.at[2], device(0, 0, 3, 0))

    def mlp(slot, count, weights, first):
        rows = 128 * count
        tokens = tok[slot:slot + count].reshape(rows, CHANNELS)
        for index, s in enumerate(weights):
            pre = dot(tokens, wa[s]) + ba[s, 0:1, :]
            hidden = (0.5 * pre * (1.0 + lax.erf(pre * (0.5 ** 0.5)))).astype(BF)
            for n in range(3):
                lanes = slice(n * 512, n * 512 + 512)
                term = dot(hidden, wb[s, :, lanes])
                if first and index == 0:
                    acc[0:rows, lanes] = term
                else:
                    acc[0:rows, lanes] += term

    def scatter(slot):
        sent = []
        for tau in (1, 3, 2):
            into = SLOT_OF[(OFFSET[slot] - tau) % 4]
            peer = SLOT_OF[(-tau) % 4] - 1
            sent.append(
                push(part.at[slot, (z + tau) % 4], rs_in.at[peer, into], device(0, 0, tau, 0))
            )
        return sent

    scale = vec_ref[3:4, :]
    mlp(0, 1, (0,), True)
    for copy in w_core:
        copy.wait()
    mlp(0, 1, (1,), False)
    for copy in w_y:
        copy.wait()
    w_fwd = [
        push(wa.at[2], wa.at[3], other), push(wb.at[2], wb.at[3], other), push(ba.at[2], ba.at[3], other),
    ]
    t_next.wait()
    t_far0 = push(tok.at[1, 0:64], tok.at[3, 0:64], device(0, 0, 1, 0))
    t_prev.wait()
    t_far1 = push(tok.at[2, 64:128], tok.at[3, 64:128], device(0, 0, 3, 0))
    mlp(0, 1, (2,), False)
    for copy in w_fwd:
        copy.wait()
    mlp(0, 1, (3,), False)
    part[0] = (acc[0:128, :] * scale + (feat[...] + scale * vec_ref[4:5, :])).astype(BF).reshape(4, 32, CHANNELS)
    scatters = scatter(0)

    for copy in red_copies:
        copy.wait()
    mine = quad.at[pl.ds(plane * 6, 6)]

    def reduce_block(g, carry):
        total = quad[plane * 6 + g].astype(F32)
        for n in range(15):
            total = total + red_in[n, g].astype(F32)
        mf[pair, plane * 6 + g] = total.astype(BF)
        return carry

    lax.fori_loop(0, 6, reduce_block, 0)
    total = quad[96].astype(F32)
    for n in range(15):
        total = total + red_bias[n, 0].astype(F32)
    mf[pair, 96] = total.astype(BF)
    block = mf.at[pair, pl.ds(plane * 6, 6)]
    all_copies = [push(block, block, device(0, dy, dz, 0)) for dy, dz in planes]

    mlp(1, 2, (0, 1, 2, 3), True)
    for slot in (1, 2):
        part[slot] = (acc[128 * slot - 128:128 * slot, :] * scale).astype(BF).reshape(4, 32, CHANNELS)
        scatters += scatter(slot)
    for copy in all_copies:
        copy.wait()
    m_next = push(mf.at[pair], mf.at[pair], device(1, 0, 0, 0))
    m_prev = push(mf.at[pair], mf.at[pair], device(3, 0, 0, 0))
    m_core = [push(mf.at[pair], mf.at[pair], other)]
    t_far0.wait()
    t_far1.wait()
    mlp(3, 1, (0, 1, 2, 3), True)
    part[3] = (acc[0:128, :] * scale).astype(BF).reshape(4, 32, CHANNELS)
    scatters += scatter(3)
    for copy in scatters:
        copy.wait()

    for slot in range(4):
        for n in range(3):
            lanes = slice(n * 512, n * 512 + 512)
            value = part[slot, z, :, lanes].astype(F32)
            for peer in range(3):
                value = value + rs_in[peer, slot, :, lanes].astype(F32)
            for q in range(4):
                stage_t[q, (z + OFFSET[slot] + 4) % 4, :, lanes] = value[8 * q:8 * q + 8]
    for q in range(4):
        stage_b[q] = stage_t[q].reshape(32, CHANNELS).astype(BF)
    my_q = ylo * 2 + core
    seq_copies = []
    for dy in range(2):
        for dk in range(2):
            if (dy, dk) != (0, 0):
                q = ((ylo + dy) % 2) * 2 + (core + dk) % 2
                seq_copies.append(push(stage_b.at[q], seq_in.at[my_q], device(0, dy * yflip, 0, dk)))
    seq_in[my_q] = stage_b[my_q]

    x_prev = ((x + 3) % 4) * 2 + core
    x_next = ((x + 1) % 4) * 2 + core
    x_far = ((x + 2) % 4) * 2 + core
    m_next.wait()
    far0 = push(mf.at[x_prev, 0:48], mf.at[x_prev, 0:48], device(1, 0, 0, 0))
    m_core.append(push(mf.at[x_prev], mf.at[x_prev], other))
    m_prev.wait()
    far1 = push(mf.at[x_next, 48:97], mf.at[x_next, 48:97], device(3, 0, 0, 0))
    m_core.append(push(mf.at[x_next], mf.at[x_next], other))
    for copy in seq_copies:
        copy.wait()
    for n in range(3):
        lanes = slice(n * 512, n * 512 + 512)
        tok[0, :, lanes] = dot(seq_ref[...], seq_in[:, :, lanes].reshape(128, 512)).astype(BF)
    for b in range(19):
        if b % 13 == 12:
            ext[:, b * 128:b * 128 + 128] = jnp.where(
                lax.broadcasted_iota(jnp.int32, (128, 128), 1) == 0, 1.0, 0.0
            )
        else:
            lanes = slice((b % 13) * 128, (b % 13) * 128 + 128)
            ext[:, b * 128:b * 128 + 128] = tok[0, :, lanes].astype(F32)
    far0.wait()
    far1.wait()
    m_core.append(push(mf.at[x_far], mf.at[x_far], other))
    for copy in m_core:
        copy.wait()

    encoded = tok[0]

    def squares_of(i, total):
        cells = tok[0, :, pl.ds(pl.multiple_of(i * 128, 128), 128)]
        groups = pl.ds(i * 8, 8)

        def other_block(d):
            return ext[:, pl.ds(pl.multiple_of((i + d) * 128, 128), 128)]

        total = total + dot(cells, mf[5, groups, :, 256:384].reshape(128, 128)) * other_block(0)
        for j in (6, 7):
            value = 2.0 * dot(cells, mf[j, groups].reshape(128, 384))
            for t in range(3):
                total = total + value[:, t * 128:t * 128 + 128] * other_block((j - 6) * 3 + t + 1)
        return total

    total = lax.fori_loop(0, BLOCKS, squares_of, jnp.zeros((128, 128), F32))
    for d in range(7):
        j, t = (17 + d) // 3, (17 + d) % 3
        weight = mf[j, 96, :, t * 128:t * 128 + 128].astype(F32)[0:1]
        total = total + (1.0 if d == 0 else 2.0) * weight * ext[:, (12 + d) * 128:(13 + d) * 128]
    squares = jnp.maximum(jnp.sum(total, axis=-1, keepdims=True), 0.0)
    inverse = lax.rsqrt(squares * (1.0 / LANGUAGE_WIDTH) + 1e-06)
    for j in range(6):
        bias = mf[j, 96].astype(F32)[0:1]
        lin[:, j * 384:j * 384 + 384] = inverse * (dot(encoded, mf[j, 0:96].reshape(CHANNELS, 384)) + bias)
    adapter_in = lin[:, 2048:2176].astype(BF)
    for n in range(8):
        lanes = slice(n * 256, n * 256 + 256)
        value = lin[:, lanes] + kvb_ref[0:1, lanes] + dot(adapter_in, up_ref[:, lanes])
        if n < 4:
            for h in range(2):
                head = value[:, h * 128:h * 128 + 128]
                turned = head * cosine + pltpu.roll(head, 64, 1) * sine
                kv_ref[:, n * 256 + h * 128:n * 256 + h * 128 + 128] = turned.astype(BF)
        else:
            kv_ref[:, lanes] = value.astype(BF)

    weighted = (inverse * adapter_grad).astype(BF)
    for n in range(3):
        value = dot_tn(encoded[:, n * 512:n * 512 + 512], weighted)
        ein[n * 32:n * 32 + 32] = value.astype(BF).reshape(32, 16, 128)
    shifted = jnp.sum(weighted.astype(F32), axis=0, keepdims=True)
    ein[96] = jnp.where(lax.broadcasted_iota(jnp.int32, (16, 128), 0) == 0, shifted, 0.0).astype(BF)
    for n in range(16):
        value = dot_tn(adapter_in, grad[:, n * 128:n * 128 + 128])
        value = value[0:64] if n < 8 else value[64:128]
        ein[97 + 4 * n:101 + 4 * n] = (0.5 * value).astype(BF).reshape(4, 16, 128)
    ein[161:176] = jnp.zeros((15, 16, 128), BF)
    sums = []
    for n, (dy, dz) in enumerate(planes):
        target_plane = ((y + dy) % 4) * 4 + (z + dz) % 4
        sums.append(push(ein.at[pl.ds(target_plane * 11, 11)], e_in1.at[n], device(0, dy, dz, 0)))
    for copy in sums:
        copy.wait()
    value = ein[pl.ds(plane * 11, 11)].astype(F32)
    for n in range(15):
        value = value + e_in1[n].astype(F32)
    e_in2[pair] = value.astype(BF)
    sums = []
    for dx in range(4):
        for dk in range(2):
            if (dx, dk) != (0, 0):
                sums.append(push(e_in2.at[pair], e_in2.at[pair], device(dx, 0, 0, dk)))
    for copy in sums:
        copy.wait()
    value = e_in2[0].astype(F32)
    for n in range(1, 8):
        value = value + e_in2[n].astype(F32)
    mine = e_all.at[pl.ds(plane * 11, 11)]
    mine[...] = value.astype(BF)
    sums = [push(mine, mine, device(0, dy, dz, 0)) for dy, dz in planes]
    for copy in sums:
        copy.wait()
    down_ref[...] = dot(pt_ref[...], e_all[0:104].reshape(EXT, 128)) * gain_ref[...]
    for n in range(16):
        lanes = slice((n % 8) * 128, (n % 8) * 128 + 128)
        upg_ref[n // 8, :, lanes] = e_all[97 + 4 * n:101 + 4 * n].reshape(64, 128).astype(F32)


def orders():
    tile = [[0.0] * 128 for _ in range(128)]
    seq = [[0.0] * 128 for _ in range(128)]
    for w in range(4):
        for h in range(8):
            for i in range(4):
                tile[(h % 4) * 32 + (h // 4) * 16 + (i // 2) * 8 + w * 2 + i % 2][w * 32 + h * 4 + i] = 1.0
    for ys in range(2):
        for cs in range(2):
            for zs in range(4):
                for w in range(4):
                    for i in range(2):
                        here = (ys * 2 + cs) * 32 + zs * 8 + w * 2 + i
                        seq[i * 64 + ys * 32 + zs * 8 + cs * 4 + w][here] = 1.0
    return jnp.array(tile, BF), jnp.array(seq, BF)


def local(
    feature_grid, depthwise_kernel, depthwise_bias, layer_norm_gain, layer_norm_shift,
    expansion_weight, expansion_bias, reduction_weight, reduction_bias, layer_branch_scale,
    projector_weight, projector_bias, input_norm_gain, key_value_weight, key_value_bias,
    adapter_down_weight, adapter_up_weight, image_start_positions, key_value_cotangent,
):
    device_block = lax.axis_index("row") * 16 + lax.axis_index("col")
    seq_index = device_block * 2 + jnp.arange(2, dtype=jnp.int32)
    match = (seq_index % IMAGES)[:, None] == jnp.arange(IMAGES, dtype=jnp.int32)[None, :]
    offsets = jnp.sum(jnp.where(match, image_start_positions[None, :], 0), axis=1)
    positions = (offsets + seq_index // IMAGES * 64)[:, None] + jnp.arange(64, dtype=jnp.int32)[None, :]
    freq_steps = jnp.arange(HEAD_DIM // 2, dtype=F32)
    inverse = jnp.exp(freq_steps * (-2.0 * math.log(ROPE_THETA) / HEAD_DIM))
    angle = positions.astype(F32).reshape(128, 1) * inverse
    cosine, sine = jnp.cos(angle), jnp.sin(angle)
    cosine = jnp.concatenate([cosine, cosine], axis=1)
    sine = jnp.concatenate([-sine, sine], axis=1)

    cells = feature_grid.transpose(2, 0, 1, 3).reshape(4, 32, CHANNELS)
    taps = depthwise_kernel.reshape(49, CHANNELS).astype(F32)
    vectors = jnp.stack(
        [depthwise_bias, layer_norm_gain, layer_norm_shift, layer_branch_scale, reduction_bias]
        + [jnp.zeros_like(depthwise_bias)] * 3
    )
    b1 = jnp.broadcast_to(expansion_bias[None, :], (8, 384))
    pt = jnp.concatenate(
        [projector_weight.T, projector_bias[:, None], jnp.zeros((64, 127), BF)], axis=1
    )
    gain = input_norm_gain.astype(F32)[:, None]
    gb = jnp.concatenate([key_value_weight, adapter_down_weight], axis=1).astype(F32) * gain
    gb = jnp.pad(gb.astype(BF), ((0, 0), (0, 896))).reshape(64, 8, 384).transpose(1, 0, 2)
    half = (adapter_up_weight.astype(F32) * 0.5).astype(BF)
    zero = jnp.zeros((64, 1024), BF)
    up = jnp.concatenate(
        [jnp.concatenate([half[0], zero], axis=1), jnp.concatenate([zero, half[1]], axis=1)], axis=0
    )
    tile_order, seq_order = orders()
    vmem = pl.BlockSpec(memory_space=pltpu.VMEM)
    kv, down, upg = pl.pallas_call(
        kernel,
        out_shape=(
            jax.ShapeDtypeStruct((128, 2048), BF),
            jax.ShapeDtypeStruct((64, 128), F32),
            jax.ShapeDtypeStruct((2, 64, 1024), F32),
        ),
        in_specs=[vmem] * 16,
        out_specs=(vmem, vmem, vmem),
        scratch_shapes=[
            pltpu.VMEM((10, 64, CHANNELS), BF),
            pltpu.VMEM((4, 32, CHANNELS), F32),
            pltpu.VMEM((4, 128, CHANNELS), BF),
            pltpu.VMEM((4, CHANNELS, 384), BF),
            pltpu.VMEM((4, 384, CHANNELS), BF),
            pltpu.VMEM((4, 8, 384), F32),
            pltpu.VMEM((128, CHANNELS), F32),
            pltpu.VMEM((256, CHANNELS), F32),
            pltpu.VMEM((4, 4, 32, CHANNELS), BF),
            pltpu.VMEM((3, 4, 32, CHANNELS), BF),
            pltpu.VMEM((4, 4, 8, CHANNELS), F32),
            pltpu.VMEM((4, 32, CHANNELS), BF),
            pltpu.VMEM((4, 32, CHANNELS), BF),
            pltpu.VMEM((8, 64, 2048), BF),
            pltpu.VMEM((104, 16, 384), BF),
            pltpu.VMEM((15, 6, 16, 384), BF),
            pltpu.VMEM((15, 1, 16, 384), BF),
            pltpu.VMEM((8, 97, 16, 384), BF),
            pltpu.VMEM((128, 19 * 128), F32),
            pltpu.VMEM((128, 2304), F32),
            pltpu.VMEM((128, 2048), BF),
            pltpu.VMEM((176, 16, 128), BF),
            pltpu.VMEM((15, 11, 16, 128), BF),
            pltpu.VMEM((8, 11, 16, 128), BF),
            pltpu.VMEM((176, 16, 128), BF),
            pltpu.SemaphoreType.DMA((COPIES,)),
            pltpu.SemaphoreType.DMA((COPIES,)),
            pltpu.SemaphoreType.DMA((6,)),
        ],
        compiler_params=pltpu.CompilerParams(
            collective_id=0, has_side_effects=True, vmem_limit_bytes=62 << 20
        ),
        cost_estimate=pl.CostEstimate(flops=8_000_000_000, bytes_accessed=30_000_000, transcendentals=0),
    )(
        cells, taps, vectors, expansion_weight, reduction_weight, b1, pt, gb, gain,
        up, cosine, sine, key_value_cotangent.reshape(128, 2048), key_value_bias[None, :], tile_order, seq_order,
    )
    return kv.reshape(2, 64, 2048), down, upg


def solution(mesh):
    in_specs = (
        P("row", None, "col", None), P(), P(), P(), P(),
        P(None, "col"), P("col"), P("col", None), P(), P(),
        P(None, ("row", "col")), P(("row", "col")), P(("row", "col")), P(("row", "col"), None), P(),
        P(("row", "col"), None), P(), P(), P(("row", "col"), None, None),
    )
    out_specs = (P(("row", "col"), None, None), P(("row", "col"), None), P())
    return jax.shard_map(local, mesh=mesh, in_specs=in_specs, out_specs=out_specs, check_vma=False)
```

time: 666 us -> 204 us (0.31)
  waiting for transfers between devices: 402 us -> 0 us
  Pallas kernels: 0 us -> 184 us
  blocking collectives: 147 us -> 0 us
  matrix products: 48.1 us -> 0 us
  other arithmetic: 21.5 us -> 3.73 us
  between operations: 16.5 us -> 0.73 us
  starting transfers between devices: 14.9 us -> 0 us
    reduce_scatter x4 -> x0, waiting for transfers between devices: 258 us -> none  [the longest x1 75.8 us: local(): lax.psum_scatter(branch_terms.astype(jnp.bfloat16), 'col', scatter_dimens...]
    pallas_call x0 -> x1, Pallas kernels: none -> 184 us  [local(): pl.pallas_call(kernel, out_shape=(jax.ShapeDtypeStruct((128, 2048), BF),...]
    psum x1 -> x0, waiting for transfers between devices: 83.2 us -> none  [local(): up_grad = lax.psum(up_weight_local, ('row', 'col'))]
    psum x1 -> x0, blocking collectives: 59.5 us -> none  [local(): squares = lax.psum(jnp.sum(projected * projected, axis=-1), 'col')]
    all_gather x2 -> x0, blocking collectives: 50.6 us -> none  [the longest x1 28.5 us: local(): lax.all_gather(adapter_down_weight, 'row', axis=0, tiled=True)]
    dot_general x12 -> x0, matrix products: 48.1 us -> none  [the longest x1 11.5 us: local(): jnp.einsum('hiwc,cf->hiwf', lax.all_gather(normed, 'col', axis=2, tiled=T...]
    all_gather x4 -> x0, waiting for transfers between devices: 44.3 us -> none  [the longest x1 44.3 us: local(): lax.all_gather(normed, 'col', axis=2, tiled=True)]
    unnamed x1 -> x0, blocking collectives: 21 us -> none
  transfers between devices with their start and end apart: 13 -> 0, of which waited for: 10 -> 0; matrix products, arithmetic and copies ran while one was open for 5% -> 0% of each run, Pallas kernels for 0% -> 0%
where the time goes in v1:
time: 204 us; the launch traced here: 203 us
  Pallas kernels  184 us (90%)
  local copies, waits for them, and re-layouts  15.3 us (8%)
  other arithmetic  3.73 us (2%)
    pallas_call x1, Pallas kernels, local(): pl.pallas_call(kernel, out_shape=(jax.ShapeDtypeStruct((128, 2048), BF),...  184 us
    another operation x8, local copies, waits for them, and re-layouts, local(): jnp.stack([depthwise_bias, layer_norm_gain, layer_norm_shift, layer_branc...  4.2 us
    unnamed x15, local copies, waits for them, and re-layouts  4.13 us

profile of v1, /device:TPU:1, one launch (start us, length us, event | category | flops | bytes accessed | tf_op | source)
XLA Modules:
  0.0 203.3 jit_solution(12676649987038074844)
XLA Ops:
  0.6 0.0 copy-start.3
  0.7 0.9 fusion.4
  1.6 0.1 add_convert_fusion
  1.6 0.1 convert_element_type.40
  1.7 0.7 convert_bitcast_fusion
  2.4 0.7 stack.21
  3.1 0.7 stack.22
  3.8 0.7 stack.23
  4.5 0.7 stack.25
  5.2 0.7 stack.24
  5.9 1.3 broadcast_in_dim.22.b1_ref
  7.2 0.7 stack.27.vec_ref
  7.9 0.8 copy.32
  8.6 0.7 copy.34.gain_ref
  9.4 1.7 concatenate.21.pt_ref
  11.0 0.0 copy-start.2
  11.0 0.0 copy-start.5
  11.0 0.3 fusion.3
  11.4 0.8 pad_maximum_fusion
  12.1 0.0 copy-done.3
  12.2 0.8 fusion.2.up_ref
  13.0 0.0 copy-done.2
  13.1 0.0 copy-done.5
  13.1 0.0 copy-start.4
  13.1 0.0 copy-start.1
  13.1 0.1 multiply_convert_fusion
  13.2 0.8 copy.38
  14.0 0.0 copy-done.4
  14.0 0.8 reshape.86.taps_ref
  14.8 0.0 copy-done.1
  14.8 0.8 copy.35.x_ref
  15.6 183.6 %shard_map.220 = (bf16[128,2048]{1,0:T(8,128)(2,1)}, f32[64,128]{1,0:T(8,128)}, f32[2,64,1024]{2,1,0:T(8,128)}) custom-call(bf16[4,32,1536]{2,1,0:T(8,128)(2,1)} %copy.35.x_ref, f32[49,1536]{1,0:T(8,128)} %reshape.86.taps_ref, f32[8,1536]{1,0:T(8,128)} %stack.27.vec_ref, bf16[1536,384]{1,0:T(8,128)(2,1)} %w1_ref.1, bf16[384,1536]{1,0:T(8,128)(2,1)} %w2_ref.1, ...), custom_call_target="tpu_custom_call" | custom-call | flops 8000000000 | bytes 30000000 | tf_op jit(solution)/shard_map/pallas_call | solution.py:500
  199.2 0.0 copy-start
  199.2 1.9 copy.42
  201.1 1.4 copy.43
  202.5 0.0 copy-done
  202.5 0.8 copy.44
  (9 shorter events, 0.1 us)
Async XLA Ops:
  0.6 11.5 %copy-start.3 = (bf16[2,64,1024]{2,1,0:T(8,128)(2,1)S(1)}, bf16[2,64,1024]{2,1,0:T(8,128)(2,1)}, u32[]{:S(2)}) copy-start(bf16[2,64,1024]{2,1,0:T(8,128)(2,1)} %param.37) | copy-start | bytes 786436
  11.0 2.0 copy-start.2
  11.0 2.0 copy-start.5
  13.1 1.0 copy-start.4
  13.1 1.8 copy-start.1
  199.2 3.3 %copy-start = (f32[2,64,1024]{2,1,0:T(8,128)S(1)}, f32[2,64,1024]{2,1,0:T(8,128)}, u32[]{:S(2)}) copy-start(f32[2,64,1024]{2,1,0:T(8,128)} %get-tuple-element.23) | copy-start | bytes 1572868

commit v2 on v1

--- a/solution.py
+++ b/solution.py
@@ -18,7 +18,7 @@
 MESH = pl.DeviceIdType.MESH
 BF = jnp.bfloat16
 F32 = jnp.float32
-COPIES = 160
+COPIES = 200
 SLOT_OF = {0: 0, 3: 1, 1: 2, 2: 3}
 OFFSET = (0, -1, 1, 2)
 
@@ -40,7 +40,7 @@
     up_ref, cos_ref, sin_ref, cot_ref, kvb_ref, perm_ref, seq_ref,
     kv_ref, down_ref, upg_ref,
     pad, conv, tok, wa, wb, ba, feat, acc, part, rs_in, stage_t, stage_b, seq_in,
-    pb, quad, red_in, red_bias, mf, ext, lin, grad,
+    pb, quad, red_z, red_mid, red_y, red_bias, mf, ext, lin, grad,
     ein, e_in1, e_in2, e_all, send, recv, lsem,
 ):
     row = lax.axis_index("row")
@@ -173,17 +173,18 @@
             around = jnp.where(shift >= 13, shift - 13, shift)
             start = jnp.where(block < 17, 13 + t, around) * 128
             right = pb[:, :, pl.ds(pl.multiple_of(start, 128), 128)].reshape(512, 128)
-            value = dot_tn(left, right).astype(BF)
-            quad[pl.ds(i * 8, 8), :, t * 128:t * 128 + 128] = value.reshape(8, 16, 128)
+            value = dot_tn(left, right).astype(BF).reshape(4, 2, 16, 128)
+            for r in range(4):
+                p = i * 4 + r
+                quad[p // 12, p % 12, :, :, t * 128:t * 128 + 128] = value[r]
         return carry
 
     lax.fori_loop(0, 13, products, 0)
     red_copies = []
-    for n, (dy, dz) in enumerate(planes):
-        target_plane = ((y + dy) % 4) * 4 + (z + dz) % 4
-        target = device(0, dy, dz, 0)
-        red_copies.append(push(quad.at[pl.ds(target_plane * 6, 6)], red_in.at[n], target))
-        red_copies.append(push(quad.at[96:97], red_bias.at[n], target))
+    for n, dz in enumerate((1, 3, 2)):
+        target = device(0, 0, dz, 0)
+        red_copies.append(push(quad.at[0:4, pl.ds(((z + dz) % 4) * 3, 3)], red_z.at[n], target))
+        red_copies.append(push(quad.at[4, 0, 0], red_bias.at[n], target))
 
     h_rt.wait()
     h_lt.wait()
@@ -263,15 +264,55 @@
     for copy in w_core:
         copy.wait()
     mlp(0, 1, (1,), False)
-    for copy in w_y:
-        copy.wait()
-    w_fwd = [
-        push(wa.at[2], wa.at[3], other), push(wb.at[2], wb.at[3], other), push(ba.at[2], ba.at[3], other),
-    ]
+
+    for copy in red_copies:
+        copy.wait()
+
+    def sum_z(n, carry):
+        h, p = n // 3, n % 3
+        total = quad[h, z * 3 + p].astype(F32)
+        for m in range(3):
+            total = total + red_z[m, h, p].astype(F32)
+        red_mid[h, p] = total.astype(BF)
+        return carry
+
+    lax.fori_loop(0, 12, sum_z, 0)
+    total = quad[4, 0, 0].astype(F32)
+    for m in range(3):
+        total = total + red_bias[m].astype(F32)
+    red_bias[6] = total.astype(BF)
+    red_copies = []
+    for n, dy in enumerate((1, 3, 2)):
+        target = device(0, dy, 0, 0)
+        red_copies.append(push(red_mid.at[(y + dy) % 4], red_y.at[n], target))
+        red_copies.append(push(red_bias.at[6], red_bias.at[3 + n], target))
     t_next.wait()
     t_far0 = push(tok.at[1, 0:64], tok.at[3, 0:64], device(0, 0, 1, 0))
     t_prev.wait()
     t_far1 = push(tok.at[2, 64:128], tok.at[3, 64:128], device(0, 0, 3, 0))
+    for copy in red_copies:
+        copy.wait()
+
+    def sum_y(p, carry):
+        total = red_mid[y, p].astype(F32)
+        for m in range(3):
+            total = total + red_y[m, p].astype(F32)
+        mf[pair, pl.ds(plane * 6 + p * 2, 2)] = total.astype(BF)
+        return carry
+
+    lax.fori_loop(0, 3, sum_y, 0)
+    total = red_bias[6].astype(F32)
+    for m in range(3):
+        total = total + red_bias[3 + m].astype(F32)
+    mf[pair, 96] = total.astype(BF)
+    block = mf.at[pair, pl.ds(plane * 6, 6)]
+    all_z = [push(block, block, device(0, 0, dz, 0)) for dz in (1, 3, 2)]
+    m_bias = [push(mf.at[pair, 96], mf.at[pair, 96], device(dx, 0, 0, 0)) for dx in (1, 3, 2)]
+    for copy in w_y:
+        copy.wait()
+    w_fwd = [
+        push(wa.at[2], wa.at[3], other), push(wb.at[2], wb.at[3], other), push(ba.at[2], ba.at[3], other),
+    ]
     mlp(0, 1, (2,), False)
     for copy in w_fwd:
         copy.wait()
@@ -279,39 +320,59 @@
     part[0] = (acc[0:128, :] * scale + (feat[...] + scale * vec_ref[4:5, :])).astype(BF).reshape(4, 32, CHANNELS)
     scatters = scatter(0)
 
-    for copy in red_copies:
-        copy.wait()
-    mine = quad.at[pl.ds(plane * 6, 6)]
-
-    def reduce_block(g, carry):
-        total = quad[plane * 6 + g].astype(F32)
-        for n in range(15):
-            total = total + red_in[n, g].astype(F32)
-        mf[pair, plane * 6 + g] = total.astype(BF)
-        return carry
-
-    lax.fori_loop(0, 6, reduce_block, 0)
-    total = quad[96].astype(F32)
-    for n in range(15):
-        total = total + red_bias[n, 0].astype(F32)
-    mf[pair, 96] = total.astype(BF)
-    block = mf.at[pair, pl.ds(plane * 6, 6)]
-    all_copies = [push(block, block, device(0, dy, dz, 0)) for dy, dz in planes]
-
+    x_prev = ((x + 3) % 4) * 2 + core
+    x_next = ((x + 1) % 4) * 2 + core
+    x_far = ((x + 2) % 4) * 2 + core
+
+    def piece(owner, dy, low=0, count=24):
+        return mf.at[owner, pl.ds(((y + dy) % 4) * 24 + low, count)]
+
+    m_core = []
+
+    def send_piece(dy):
+        sent = [
+            push(piece(pair, dy), piece(pair, dy), device(1, 0, 0, 0)),
+            push(piece(pair, dy), piece(pair, dy), device(3, 0, 0, 0)),
+        ]
+        m_core.append(push(piece(pair, dy), piece(pair, dy), other))
+        return sent
+
+    def relay_piece(dy, sent):
+        sent[0].wait()
+        far = [push(piece(x_prev, dy, 0, 12), piece(x_prev, dy, 0, 12), device(1, 0, 0, 0))]
+        m_core.append(push(piece(x_prev, dy), piece(x_prev, dy), other))
+        sent[1].wait()
+        far.append(push(piece(x_next, dy, 12, 12), piece(x_next, dy, 12, 12), device(3, 0, 0, 0)))
+        m_core.append(push(piece(x_next, dy), piece(x_next, dy), other))
+        return far
+
+    def finish_piece(dy, far):
+        far[0].wait()
+        far[1].wait()
+        m_core.append(push(piece(x_far, dy), piece(x_far, dy), other))
+
+    for copy in all_z:
+        copy.wait()
+    all_y = [push(piece(pair, 0), piece(pair, 0), device(0, dy, 0, 0)) for dy in (1, 3, 2)]
+    sent_0 = send_piece(0)
     mlp(1, 2, (0, 1, 2, 3), True)
     for slot in (1, 2):
         part[slot] = (acc[128 * slot - 128:128 * slot, :] * scale).astype(BF).reshape(4, 32, CHANNELS)
         scatters += scatter(slot)
-    for copy in all_copies:
-        copy.wait()
-    m_next = push(mf.at[pair], mf.at[pair], device(1, 0, 0, 0))
-    m_prev = push(mf.at[pair], mf.at[pair], device(3, 0, 0, 0))
-    m_core = [push(mf.at[pair], mf.at[pair], other)]
+    all_y[0].wait()
+    sent_3 = send_piece(3)
+    far_0 = relay_piece(0, sent_0)
     t_far0.wait()
     t_far1.wait()
     mlp(3, 1, (0, 1, 2, 3), True)
     part[3] = (acc[0:128, :] * scale).astype(BF).reshape(4, 32, CHANNELS)
     scatters += scatter(3)
+    all_y[1].wait()
+    sent_1 = send_piece(1)
+    all_y[2].wait()
+    sent_2 = send_piece(2)
+    finish_piece(0, far_0)
+    far_3 = relay_piece(3, sent_3)
     for copy in scatters:
         copy.wait()
 
@@ -334,15 +395,6 @@
                 seq_copies.append(push(stage_b.at[q], seq_in.at[my_q], device(0, dy * yflip, 0, dk)))
     seq_in[my_q] = stage_b[my_q]
 
-    x_prev = ((x + 3) % 4) * 2 + core
-    x_next = ((x + 1) % 4) * 2 + core
-    x_far = ((x + 2) % 4) * 2 + core
-    m_next.wait()
-    far0 = push(mf.at[x_prev, 0:48], mf.at[x_prev, 0:48], device(1, 0, 0, 0))
-    m_core.append(push(mf.at[x_prev], mf.at[x_prev], other))
-    m_prev.wait()
-    far1 = push(mf.at[x_next, 48:97], mf.at[x_next, 48:97], device(3, 0, 0, 0))
-    m_core.append(push(mf.at[x_next], mf.at[x_next], other))
     for copy in seq_copies:
         copy.wait()
     for n in range(3):
@@ -356,9 +408,15 @@
         else:
             lanes = slice((b % 13) * 128, (b % 13) * 128 + 128)
             ext[:, b * 128:b * 128 + 128] = tok[0, :, lanes].astype(F32)
-    far0.wait()
-    far1.wait()
-    m_core.append(push(mf.at[x_far], mf.at[x_far], other))
+    far_1 = relay_piece(1, sent_1)
+    finish_piece(3, far_3)
+    far_2 = relay_piece(2, sent_2)
+    finish_piece(1, far_1)
+    for copy in m_bias:
+        copy.wait()
+    for owner in (pair, x_prev, x_next, x_far):
+        m_core.append(push(mf.at[owner, 96], mf.at[owner, 96], other))
+    finish_piece(2, far_2)
     for copy in m_core:
         copy.wait()
 
@@ -521,9 +579,11 @@
             pltpu.VMEM((4, 32, CHANNELS), BF),
             pltpu.VMEM((4, 32, CHANNELS), BF),
             pltpu.VMEM((8, 64, 2048), BF),
-            pltpu.VMEM((104, 16, 384), BF),
-            pltpu.VMEM((15, 6, 16, 384), BF),
-            pltpu.VMEM((15, 1, 16, 384), BF),
+            pltpu.VMEM((5, 12, 2, 16, 384), BF),
+            pltpu.VMEM((3, 4, 3, 2, 16, 384), BF),
+            pltpu.VMEM((4, 3, 2, 16, 384), BF),
+            pltpu.VMEM((3, 3, 2, 16, 384), BF),
+            pltpu.VMEM((7, 16, 384), BF),
             pltpu.VMEM((8, 97, 16, 384), BF),
             pltpu.VMEM((128, 19 * 128), F32),
             pltpu.VMEM((128, 2304), F32),

time: 204 us -> 183 us (0.90)
  Pallas kernels: 184 us -> 163 us
    pallas_call x1, Pallas kernels: 184 us -> 163 us  [local(): pl.pallas_call(kernel, out_shape=(jax.ShapeDtypeStruct((128, 2048), BF),...]
where the time goes in v2:
time: 183 us; the launch traced here: 182 us
  Pallas kernels  163 us (89%)
  local copies, waits for them, and re-layouts  15.3 us (8%)
  other arithmetic  3.73 us (2%)
    pallas_call x1, Pallas kernels, local(): pl.pallas_call(kernel, out_shape=(jax.ShapeDtypeStruct((128, 2048), BF),...  163 us
    another operation x8, local copies, waits for them, and re-layouts, local(): jnp.stack([depthwise_bias, layer_norm_gain, layer_norm_shift, layer_branc...  4.2 us
    unnamed x15, local copies, waits for them, and re-layouts  4.13 us

profile of v2, /device:TPU:1, one launch (start us, length us, event | category | flops | bytes accessed | tf_op | source)
XLA Modules:
  0.0 182.3 jit_solution(7173562747611095881)
XLA Ops:
  0.6 0.0 copy-start.3
  0.7 0.9 fusion.4
  1.6 0.1 add_convert_fusion
  1.6 0.1 convert_element_type.40
  1.7 0.7 convert_bitcast_fusion
  2.4 0.7 stack.21
  3.1 0.7 stack.22
  3.8 0.7 stack.23
  4.5 0.7 stack.25
  5.2 0.7 stack.24
  5.9 1.3 broadcast_in_dim.22.b1_ref
  7.2 0.7 stack.27.vec_ref
  7.9 0.8 copy.32
  8.6 0.7 copy.34.gain_ref
  9.4 1.7 concatenate.21.pt_ref
  11.0 0.0 copy-start.2
  11.0 0.0 copy-start.5
  11.0 0.3 fusion.3
  11.4 0.8 pad_maximum_fusion
  12.1 0.0 copy-done.3
  12.2 0.8 fusion.2.up_ref
  13.0 0.0 copy-done.2
  13.1 0.0 copy-done.5
  13.1 0.0 copy-start.4
  13.1 0.0 copy-start.1
  13.1 0.1 multiply_convert_fusion
  13.2 0.8 copy.38
  14.0 0.0 copy-done.4
  14.0 0.8 reshape.86.taps_ref
  14.8 0.0 copy-done.1
  14.8 0.8 copy.35.x_ref
  15.6 162.5 %shard_map.220 = (bf16[128,2048]{1,0:T(8,128)(2,1)}, f32[64,128]{1,0:T(8,128)}, f32[2,64,1024]{2,1,0:T(8,128)}) custom-call(bf16[4,32,1536]{2,1,0:T(8,128)(2,1)} %copy.35.x_ref, f32[49,1536]{1,0:T(8,128)} %reshape.86.taps_ref, f32[8,1536]{1,0:T(8,128)} %stack.27.vec_ref, bf16[1536,384]{1,0:T(8,128)(2,1)} %w1_ref.1, bf16[384,1536]{1,0:T(8,128)(2,1)} %w2_ref.1, ...), custom_call_target="tpu_custom_call" | custom-call | flops 8000000000 | bytes 30000000 | tf_op jit(solution)/shard_map/pallas_call | solution.py:558
  178.1 0.0 copy-start
  178.2 1.9 %copy.42 = bf16[2,64,2048]{2,1,0:T(8,128)(2,1)} copy(bf16[2,64,2048]{2,1,0:T(8,128)(2,1)} %bitcast.22) | data formatting | bytes 1048576
  180.1 1.4 copy.43
  181.5 0.0 copy-done
  181.5 0.8 copy.44
  (9 shorter events, 0.1 us)
Async XLA Ops:
  0.6 11.5 %copy-start.3 = (bf16[2,64,1024]{2,1,0:T(8,128)(2,1)S(1)}, bf16[2,64,1024]{2,1,0:T(8,128)(2,1)}, u32[]{:S(2)}) copy-start(bf16[2,64,1024]{2,1,0:T(8,128)(2,1)} %param.37) | copy-start | bytes 786436
  11.0 2.0 %copy-start.2 = (bf16[64,2048]{1,0:T(8,128)(2,1)S(1)}, bf16[64,2048]{1,0:T(8,128)(2,1)}, u32[]{:S(2)}) copy-start(bf16[64,2048]{1,0:T(8,128)(2,1)} %param.34) | copy-start | bytes 786436
  11.0 2.0 %copy-start.5 = (bf16[64,128]{1,0:T(8,128)(2,1)S(1)}, bf16[64,128]{1,0:T(8,128)(2,1)}, u32[]{:S(2)}) copy-start(bf16[64,128]{1,0:T(8,128)(2,1)} %param.36) | copy-start | bytes 49156
  13.1 1.0 copy-start.4
  13.1 1.8 copy-start.1
  178.1 3.3 %copy-start = (f32[2,64,1024]{2,1,0:T(8,128)S(1)}, f32[2,64,1024]{2,1,0:T(8,128)}, u32[]{:S(2)}) copy-start(f32[2,64,1024]{2,1,0:T(8,128)} %get-tuple-element.23) | copy-start | bytes 1572868

commit v3 on v2

--- a/solution.py
+++ b/solution.py
@@ -3,6 +3,7 @@
 
 import jax
 import jax.numpy as jnp
+import numpy as np
 from jax import lax
 from jax.experimental import pallas as pl
 from jax.experimental.pallas import tpu as pltpu
@@ -36,12 +37,14 @@
 
 
 def kernel(
-    x_ref, taps_ref, vec_ref, w1_ref, w2_ref, b1_ref, pt_ref, gb_ref, gain_ref,
-    up_ref, cos_ref, sin_ref, cot_ref, kvb_ref, perm_ref, seq_ref,
+    x_ref, depth_ref, dbias_ref, lgain_ref, lshift_ref, w1_ref, w2_ref, b1_ref, rbias_ref, scale_ref,
+    proj_ref, pbias_ref, ngain_ref, kvw_ref, kvb_ref, downw_ref, upw_ref, start_ref, cot_ref,
+    freq_ref, perm_ref, seq_ref,
     kv_ref, down_ref, upg_ref,
     pad, conv, tok, wa, wb, ba, feat, acc, part, rs_in, stage_t, stage_b, seq_in,
     pb, quad, red_z, red_mid, red_y, red_bias, mf, ext, lin, grad,
-    ein, e_in1, e_in2, e_all, send, recv, lsem,
+    ein, e_core, e_mid, e_in1, e_in2, e_all, pt_ref, gb_ref, up_ref, taps_ref, cos_ref, sin_ref,
+    send, recv, lsem,
 ):
     row = lax.axis_index("row")
     col = lax.axis_index("col")
@@ -88,6 +91,20 @@
     barrier = pltpu.get_barrier_semaphore()
     for partner in partners:
         pl.semaphore_signal(barrier, inc=1, device_id=partner, device_id_type=MESH)
+    diagonal = lax.broadcasted_iota(jnp.int32, (64, 64), 0) == lax.broadcasted_iota(jnp.int32, (64, 64), 1)
+    gain = jnp.sum(jnp.where(diagonal, ngain_ref[...].astype(F32), 0.0), axis=1, keepdims=True)
+    bias = jnp.sum(jnp.where(diagonal, pbias_ref[...].astype(F32), 0.0), axis=1, keepdims=True)
+    eye = jnp.where(diagonal, 1.0, 0.0).astype(BF)
+    for n in range(3):
+        pt_ref[:, n * 512:n * 512 + 512] = dot_nt(eye, proj_ref[n * 512:n * 512 + 512, :]).astype(BF)
+    first_lane = lax.broadcasted_iota(jnp.int32, (64, 128), 1) == 0
+    pt_ref[:, CHANNELS:EXT] = jnp.where(first_lane, bias, 0.0).astype(BF)
+    for j in range(5):
+        gb_ref[j] = (kvw_ref[:, j * 384:j * 384 + 384].astype(F32) * gain).astype(BF)
+    gb_ref[5, :, 0:128] = (kvw_ref[:, 1920:2048].astype(F32) * gain).astype(BF)
+    gb_ref[5, :, 128:256] = (downw_ref[...].astype(F32) * gain).astype(BF)
+    gb_ref[5, :, 256:384] = jnp.zeros((64, 128), BF)
+    gb_ref[6:8] = jnp.zeros((2, 64, 384), BF)
     copies0 = [
         pltpu.make_async_copy(x_ref, pad.at[3:7, 16:48], lsem.at[0]),
         pltpu.make_async_copy(w1_ref, wa.at[0], lsem.at[1]),
@@ -125,6 +142,19 @@
         push(b1_ref, ba.at[2], device(0, 1, 0, 0)),
     ]
 
+    token = lax.broadcasted_iota(jnp.int32, (128, 128), 0)
+    later = token >= 64
+    start = jnp.where(later, start_ref[core * 2 + 1], start_ref[core * 2])
+    position = start + (row * 8 + col // 2) * 64 + jnp.where(later, token - 64, token)
+    angle = position.astype(F32) * freq_ref[...]
+    cos_ref[...] = jnp.cos(angle)
+    upper = lax.broadcasted_iota(jnp.int32, (128, 128), 1) >= 64
+    sin_ref[...] = jnp.where(upper, 1.0, -1.0) * jnp.sin(angle)
+    up_ref[...] = jnp.zeros((128, 2048), BF)
+    up_ref[0:64, 0:1024] = (upw_ref[0].astype(F32) * 0.5).astype(BF)
+    up_ref[64:128, 1024:2048] = (upw_ref[1].astype(F32) * 0.5).astype(BF)
+    for a in range(7):
+        taps_ref[a, 0:7, :] = depth_ref[a].astype(F32)
     cosine = cos_ref[...]
     sine = sin_ref[...]
     for head in range(8):
@@ -201,7 +231,7 @@
 
     def conv_lanes(n, carry):
         lanes = pl.ds(pl.multiple_of(n * 128, 128), 128)
-        sums = [jnp.zeros((32, 128), F32) + vec_ref[0:1, lanes] for _ in range(4)]
+        sums = [jnp.zeros((32, 128), F32) + dbias_ref[0:1, lanes] for _ in range(4)]
         for wp in range(10):
             full = pad[wp, :, lanes].astype(F32)
             moved = pltpu.roll(full, 60, 0)
@@ -209,8 +239,7 @@
                 start = 4 * (a + 1)
                 window = full[start:start + 32] if a % 2 else moved[start - 4:start + 28]
                 for w in range(max(0, wp - 6), min(3, wp) + 1):
-                    tap = a * 7 + wp - w
-                    sums[w] = sums[w] + window * taps_ref[tap:tap + 1, lanes]
+                    sums[w] = sums[w] + window * taps_ref[a, wp - w:wp - w + 1, lanes]
         for w in range(4):
             conv[w, :, lanes] = sums[w]
         return carry
@@ -224,7 +253,7 @@
         center = jnp.sum(value, axis=-1, keepdims=True) * (1.0 / CHANNELS)
         centered = value - center
         variance = jnp.sum(centered * centered, axis=-1, keepdims=True) * (1.0 / CHANNELS)
-        value = centered * lax.rsqrt(variance + 1e-06) * vec_ref[1:2, :] + vec_ref[2:3, :]
+        value = centered * lax.rsqrt(variance + 1e-06) * lgain_ref[...] + lshift_ref[...]
         part[0, w, rows, :] = value.astype(BF)
         return carry
 
@@ -239,7 +268,7 @@
         rows = 128 * count
         tokens = tok[slot:slot + count].reshape(rows, CHANNELS)
         for index, s in enumerate(weights):
-            pre = dot(tokens, wa[s]) + ba[s, 0:1, :]
+            pre = dot(tokens, wa[s]) + ba[s]
             hidden = (0.5 * pre * (1.0 + lax.erf(pre * (0.5 ** 0.5)))).astype(BF)
             for n in range(3):
                 lanes = slice(n * 512, n * 512 + 512)
@@ -259,7 +288,7 @@
             )
         return sent
 
-    scale = vec_ref[3:4, :]
+    scale = scale_ref[...]
     mlp(0, 1, (0,), True)
     for copy in w_core:
         copy.wait()
@@ -317,7 +346,7 @@
     for copy in w_fwd:
         copy.wait()
     mlp(0, 1, (3,), False)
-    part[0] = (acc[0:128, :] * scale + (feat[...] + scale * vec_ref[4:5, :])).astype(BF).reshape(4, 32, CHANNELS)
+    part[0] = (acc[0:128, :] * scale + (feat[...] + scale * rbias_ref[...])).astype(BF).reshape(4, 32, CHANNELS)
     scatters = scatter(0)
 
     x_prev = ((x + 3) % 4) * 2 + core
@@ -444,8 +473,8 @@
     squares = jnp.maximum(jnp.sum(total, axis=-1, keepdims=True), 0.0)
     inverse = lax.rsqrt(squares * (1.0 / LANGUAGE_WIDTH) + 1e-06)
     for j in range(6):
-        bias = mf[j, 96].astype(F32)[0:1]
-        lin[:, j * 384:j * 384 + 384] = inverse * (dot(encoded, mf[j, 0:96].reshape(CHANNELS, 384)) + bias)
+        offset = mf[j, 96].astype(F32)[0:1]
+        lin[:, j * 384:j * 384 + 384] = inverse * (dot(encoded, mf[j, 0:96].reshape(CHANNELS, 384)) + offset)
     adapter_in = lin[:, 2048:2176].astype(BF)
     for n in range(8):
         lanes = slice(n * 256, n * 256 + 256)
@@ -459,45 +488,62 @@
             kv_ref[:, lanes] = value.astype(BF)
 
     weighted = (inverse * adapter_grad).astype(BF)
+
+    def place(group, value):
+        ein[group // 80, group % 80 // 5, group % 5] = value
+
     for n in range(3):
-        value = dot_tn(encoded[:, n * 512:n * 512 + 512], weighted)
-        ein[n * 32:n * 32 + 32] = value.astype(BF).reshape(32, 16, 128)
-    shifted = jnp.sum(weighted.astype(F32), axis=0, keepdims=True)
-    ein[96] = jnp.where(lax.broadcasted_iota(jnp.int32, (16, 128), 0) == 0, shifted, 0.0).astype(BF)
+        value = dot_tn(encoded[:, n * 512:n * 512 + 512], weighted).astype(BF).reshape(32, 16, 128)
+        for g in range(32):
+            place(n * 32 + g, value[g])
     for n in range(16):
         value = dot_tn(adapter_in, grad[:, n * 128:n * 128 + 128])
         value = value[0:64] if n < 8 else value[64:128]
-        ein[97 + 4 * n:101 + 4 * n] = (0.5 * value).astype(BF).reshape(4, 16, 128)
-    ein[161:176] = jnp.zeros((15, 16, 128), BF)
+        value = (0.5 * value).astype(BF).reshape(4, 16, 128)
+        for g in range(4):
+            place(96 + 4 * n + g, value[g])
+    shifted = jnp.sum(weighted.astype(F32), axis=0, keepdims=True)
+    shifted = jnp.where(lax.broadcasted_iota(jnp.int32, (16, 128), 0) == 0, shifted, 0.0).astype(BF)
+    for half in range(2):
+        for p in range(16):
+            ein[half, p, 5] = shifted
+    push(ein.at[1 - core], e_core, other).wait()
+
+    def sum_cores(p, carry):
+        e_mid[p] = (ein[core, p].astype(F32) + e_core[p].astype(F32)).astype(BF)
+        return carry
+
+    lax.fori_loop(0, 16, sum_cores, 0)
     sums = []
     for n, (dy, dz) in enumerate(planes):
         target_plane = ((y + dy) % 4) * 4 + (z + dz) % 4
-        sums.append(push(ein.at[pl.ds(target_plane * 11, 11)], e_in1.at[n], device(0, dy, dz, 0)))
+        sums.append(push(e_mid.at[target_plane], e_in1.at[n], device(0, dy, dz, 0)))
     for copy in sums:
         copy.wait()
-    value = ein[pl.ds(plane * 11, 11)].astype(F32)
+    value = e_mid[plane].astype(F32)
     for n in range(15):
         value = value + e_in1[n].astype(F32)
-    e_in2[pair] = value.astype(BF)
-    sums = []
-    for dx in range(4):
-        for dk in range(2):
-            if (dx, dk) != (0, 0):
-                sums.append(push(e_in2.at[pair], e_in2.at[pair], device(dx, 0, 0, dk)))
+    e_in2[x] = value.astype(BF)
+    sums = [push(e_in2.at[x], e_in2.at[x], device(dx, 0, 0, 0)) for dx in (1, 3, 2)]
     for copy in sums:
         copy.wait()
     value = e_in2[0].astype(F32)
-    for n in range(1, 8):
+    for n in range(1, 4):
         value = value + e_in2[n].astype(F32)
-    mine = e_all.at[pl.ds(plane * 11, 11)]
-    mine[...] = value.astype(BF)
+    value = value.astype(BF)
+    mine = e_all.at[pl.ds(core * 80 + plane * 5, 5)]
+    mine[...] = value[0:5]
     sums = [push(mine, mine, device(0, dy, dz, 0)) for dy, dz in planes]
     for copy in sums:
         copy.wait()
-    down_ref[...] = dot(pt_ref[...], e_all[0:104].reshape(EXT, 128)) * gain_ref[...]
+    mine = e_all.at[pl.ds(core * 80, 80)]
+    push(mine, mine, other).wait()
+    total_shift = value[5].astype(F32)[0:1]
+    down = dot(pt_ref[:, 0:CHANNELS], e_all[0:96].reshape(CHANNELS, 128))
+    down_ref[...] = (down + bias * total_shift) * gain
     for n in range(16):
         lanes = slice((n % 8) * 128, (n % 8) * 128 + 128)
-        upg_ref[n // 8, :, lanes] = e_all[97 + 4 * n:101 + 4 * n].reshape(64, 128).astype(F32)
+        upg_ref[n // 8, :, lanes] = e_all[96 + 4 * n:100 + 4 * n].reshape(64, 128).astype(F32)
 
 
 def orders():
@@ -523,36 +569,9 @@
     projector_weight, projector_bias, input_norm_gain, key_value_weight, key_value_bias,
     adapter_down_weight, adapter_up_weight, image_start_positions, key_value_cotangent,
 ):
-    device_block = lax.axis_index("row") * 16 + lax.axis_index("col")
-    seq_index = device_block * 2 + jnp.arange(2, dtype=jnp.int32)
-    match = (seq_index % IMAGES)[:, None] == jnp.arange(IMAGES, dtype=jnp.int32)[None, :]
-    offsets = jnp.sum(jnp.where(match, image_start_positions[None, :], 0), axis=1)
-    positions = (offsets + seq_index // IMAGES * 64)[:, None] + jnp.arange(64, dtype=jnp.int32)[None, :]
-    freq_steps = jnp.arange(HEAD_DIM // 2, dtype=F32)
-    inverse = jnp.exp(freq_steps * (-2.0 * math.log(ROPE_THETA) / HEAD_DIM))
-    angle = positions.astype(F32).reshape(128, 1) * inverse
-    cosine, sine = jnp.cos(angle), jnp.sin(angle)
-    cosine = jnp.concatenate([cosine, cosine], axis=1)
-    sine = jnp.concatenate([-sine, sine], axis=1)
-
     cells = feature_grid.transpose(2, 0, 1, 3).reshape(4, 32, CHANNELS)
-    taps = depthwise_kernel.reshape(49, CHANNELS).astype(F32)
-    vectors = jnp.stack(
-        [depthwise_bias, layer_norm_gain, layer_norm_shift, layer_branch_scale, reduction_bias]
-        + [jnp.zeros_like(depthwise_bias)] * 3
-    )
-    b1 = jnp.broadcast_to(expansion_bias[None, :], (8, 384))
-    pt = jnp.concatenate(
-        [projector_weight.T, projector_bias[:, None], jnp.zeros((64, 127), BF)], axis=1
-    )
-    gain = input_norm_gain.astype(F32)[:, None]
-    gb = jnp.concatenate([key_value_weight, adapter_down_weight], axis=1).astype(F32) * gain
-    gb = jnp.pad(gb.astype(BF), ((0, 0), (0, 896))).reshape(64, 8, 384).transpose(1, 0, 2)
-    half = (adapter_up_weight.astype(F32) * 0.5).astype(BF)
-    zero = jnp.zeros((64, 1024), BF)
-    up = jnp.concatenate(
-        [jnp.concatenate([half[0], zero], axis=1), jnp.concatenate([zero, half[1]], axis=1)], axis=0
-    )
+    freq = np.exp(np.arange(HEAD_DIM // 2, dtype=np.float32) * np.float32(-2.0 * math.log(ROPE_THETA) / HEAD_DIM))
+    freq = jnp.array(np.concatenate([freq, freq])[None, :], F32)
     tile_order, seq_order = orders()
     vmem = pl.BlockSpec(memory_space=pltpu.VMEM)
     kv, down, upg = pl.pallas_call(
@@ -562,7 +581,7 @@
             jax.ShapeDtypeStruct((64, 128), F32),
             jax.ShapeDtypeStruct((2, 64, 1024), F32),
         ),
-        in_specs=[vmem] * 16,
+        in_specs=[vmem] * 17 + [pl.BlockSpec(memory_space=pltpu.SMEM)] + [vmem] * 4,
         out_specs=(vmem, vmem, vmem),
         scratch_shapes=[
             pltpu.VMEM((10, 64, CHANNELS), BF),
@@ -570,7 +589,7 @@
             pltpu.VMEM((4, 128, CHANNELS), BF),
             pltpu.VMEM((4, CHANNELS, 384), BF),
             pltpu.VMEM((4, 384, CHANNELS), BF),
-            pltpu.VMEM((4, 8, 384), F32),
+            pltpu.VMEM((4, 1, 384), F32),
             pltpu.VMEM((128, CHANNELS), F32),
             pltpu.VMEM((256, CHANNELS), F32),
             pltpu.VMEM((4, 4, 32, CHANNELS), BF),
@@ -588,10 +607,18 @@
             pltpu.VMEM((128, 19 * 128), F32),
             pltpu.VMEM((128, 2304), F32),
             pltpu.VMEM((128, 2048), BF),
-            pltpu.VMEM((176, 16, 128), BF),
-            pltpu.VMEM((15, 11, 16, 128), BF),
-            pltpu.VMEM((8, 11, 16, 128), BF),
-            pltpu.VMEM((176, 16, 128), BF),
+            pltpu.VMEM((2, 16, 6, 16, 128), BF),
+            pltpu.VMEM((16, 6, 16, 128), BF),
+            pltpu.VMEM((16, 6, 16, 128), BF),
+            pltpu.VMEM((15, 6, 16, 128), BF),
+            pltpu.VMEM((4, 6, 16, 128), BF),
+            pltpu.VMEM((160, 16, 128), BF),
+            pltpu.VMEM((64, EXT), BF),
+            pltpu.VMEM((8, 64, 384), BF),
+            pltpu.VMEM((128, 2048), BF),
+            pltpu.VMEM((7, 8, CHANNELS), F32),
+            pltpu.VMEM((128, 128), F32),
+            pltpu.VMEM((128, 128), F32),
             pltpu.SemaphoreType.DMA((COPIES,)),
             pltpu.SemaphoreType.DMA((COPIES,)),
             pltpu.SemaphoreType.DMA((6,)),
@@ -601,8 +628,11 @@
         ),
         cost_estimate=pl.CostEstimate(flops=8_000_000_000, bytes_accessed=30_000_000, transcendentals=0),
     )(
-        cells, taps, vectors, expansion_weight, reduction_weight, b1, pt, gb, gain,
-        up, cosine, sine, key_value_cotangent.reshape(128, 2048), key_value_bias[None, :], tile_order, seq_order,
+        cells, depthwise_kernel, depthwise_bias[None, :], layer_norm_gain[None, :], layer_norm_shift[None, :],
+        expansion_weight, reduction_weight, expansion_bias[None, :], reduction_bias[None, :],
+        layer_branch_scale[None, :], projector_weight, projector_bias[None, :], input_norm_gain[None, :],
+        key_value_weight, key_value_bias[None, :], adapter_down_weight, adapter_up_weight,
+        image_start_positions, key_value_cotangent.reshape(128, 2048), freq, tile_order, seq_order,
     )
     return kv.reshape(2, 64, 2048), down, upg
 

time: 183 us -> 166 us (0.907)
  Pallas kernels: 163 us -> 149 us
  other arithmetic: 3.73 us -> 0 us
    pallas_call x1, Pallas kernels: 163 us -> 149 us  [local(): pl.pallas_call(kernel, out_shape=(jax.ShapeDtypeStruct((128, 2048), BF),...]
    broadcast_in_dim x4 -> x6, local copies, waits for them, and re-layouts: 2.75 us -> 7.72 us  [the longest x1 1.3 us: local(): layer_norm_shift[None, :]]
    another operation x8 -> x0, local copies, waits for them, and re-layouts: 4.2 us -> none  [local(): jnp.stack([depthwise_bias, layer_norm_gain, layer_norm_shift, layer_branc...]
    unnamed x15 -> x6, local copies, waits for them, and re-layouts: 4.13 us -> 5.96 us
where the time goes in v3:
time: 166 us; the launch traced here: 165 us
  Pallas kernels  149 us (90%)
  local copies, waits for them, and re-layouts  15.5 us (9%)
    pallas_call x1, Pallas kernels, local(): pl.pallas_call(kernel, out_shape=(jax.ShapeDtypeStruct((128, 2048), BF),...  149 us
    unnamed x6, local copies, waits for them, and re-layouts  5.96 us

profile of v3, /device:TPU:1, one launch (start us, length us, event | category | flops | bytes accessed | tf_op | source)
XLA Modules:
  0.0 165.4 jit_solution(15016013605928444515)
XLA Ops:
  0.6 1.3 broadcast_in_dim.30.b1_ref
  1.9 1.3 broadcast_in_dim.27.dbias_ref
  3.2 1.3 broadcast_in_dim.28.lgain_ref
  4.5 1.3 broadcast_in_dim.29.lshift_ref
  5.8 1.3 broadcast_in_dim.31.rbias_ref
  7.1 1.3 broadcast_in_dim.32.scale_ref
  8.4 1.8 %copy.27.x_ref = bf16[4,32,1536]{2,1,0:T(8,128)(2,1)} copy(bf16[4,32,1536]{2,0,1:T(4,128)(2,1)} %bitcast.9) | data formatting | bytes 786432 | tf_op jit(solution)/shard_map/reshape | solution.py:572
  10.2 1.8 %copy.26.proj_ref = bf16[1536,64]{1,0:T(8,128)(2,1)} copy(bf16[1536,64]{0,1:T(8,128)(2,1)} %param.32) | data formatting | bytes 393216 | tf_op args[10]
  12.0 149.3 %shard_map.229 = (bf16[128,2048]{1,0:T(8,128)(2,1)}, f32[64,128]{1,0:T(8,128)}, f32[2,64,1024]{2,1,0:T(8,128)}) custom-call(bf16[4,32,1536]{2,1,0:T(8,128)(2,1)} %copy.27.x_ref, bf16[7,7,1536]{2,1,0:T(8,128)(2,1)} %depth_ref.1, f32[1,1536]{1,0:T(1,128)} %broadcast_in_dim.27.dbias_ref, f32[1,1536]{1,0:T(1,128)} %broadcast_in_dim.28.lgain_ref, ...), custom_call_target="tpu_custom_call" | custom-call | flops 8000000000 | bytes 30000000 | tf_op jit(solution)/shard_map/pallas_call | solution.py:577
  161.3 0.0 copy-start
  161.3 1.9 %copy.31 = bf16[2,64,2048]{2,1,0:T(8,128)(2,1)} copy(bf16[2,64,2048]{2,1,0:T(8,128)(2,1)} %bitcast.8) | data formatting | bytes 1048576
  163.3 1.4 copy.32
  164.7 0.0 copy-done
  164.7 0.8 copy.33
Async XLA Ops:
  161.3 3.3 %copy-start = (f32[2,64,1024]{2,1,0:T(8,128)S(1)}, f32[2,64,1024]{2,1,0:T(8,128)}, u32[]{:S(2)}) copy-start(f32[2,64,1024]{2,1,0:T(8,128)} %get-tuple-element.14) | copy-start | bytes 1572868

commit v4 on v3

--- a/solution.py
+++ b/solution.py
@@ -19,7 +19,7 @@
 MESH = pl.DeviceIdType.MESH
 BF = jnp.bfloat16
 F32 = jnp.float32
-COPIES = 200
+COPIES = 240
 SLOT_OF = {0: 0, 3: 1, 1: 2, 2: 3}
 OFFSET = (0, -1, 1, 2)
 
@@ -42,8 +42,9 @@
     freq_ref, perm_ref, seq_ref,
     kv_ref, down_ref, upg_ref,
     pad, conv, tok, wa, wb, ba, feat, acc, part, rs_in, stage_t, stage_b, seq_in,
-    pb, quad, red_z, red_mid, red_y, red_bias, mf, ext, lin, grad,
-    ein, e_core, e_mid, e_in1, e_in2, e_all, pt_ref, gb_ref, up_ref, taps_ref, cos_ref, sin_ref,
+    pb, quad_a, red_z_a, red_mid_a, red_y_a, red_bias_a, mf_a,
+    quad_b, red_z_b, red_mid_b, red_y_b, red_bias_b, mf_b, ext, grad,
+    ein, e_core, e_mid, e_in1, e_in2, e_all, pt_ref, gb_ref, up_ref, taps_ref, cos_ref, sin_ref, own_b1,
     send, recv, lsem,
 ):
     row = lax.axis_index("row")
@@ -94,22 +95,19 @@
     diagonal = lax.broadcasted_iota(jnp.int32, (64, 64), 0) == lax.broadcasted_iota(jnp.int32, (64, 64), 1)
     gain = jnp.sum(jnp.where(diagonal, ngain_ref[...].astype(F32), 0.0), axis=1, keepdims=True)
     bias = jnp.sum(jnp.where(diagonal, pbias_ref[...].astype(F32), 0.0), axis=1, keepdims=True)
-    eye = jnp.where(diagonal, 1.0, 0.0).astype(BF)
-    for n in range(3):
-        pt_ref[:, n * 512:n * 512 + 512] = dot_nt(eye, proj_ref[n * 512:n * 512 + 512, :]).astype(BF)
+    pt_ref[:, 0:CHANNELS] = proj_ref[...]
+    own_b1[...] = b1_ref[...].reshape(1, 384)
     first_lane = lax.broadcasted_iota(jnp.int32, (64, 128), 1) == 0
     pt_ref[:, CHANNELS:EXT] = jnp.where(first_lane, bias, 0.0).astype(BF)
-    for j in range(5):
-        gb_ref[j] = (kvw_ref[:, j * 384:j * 384 + 384].astype(F32) * gain).astype(BF)
-    gb_ref[5, :, 0:128] = (kvw_ref[:, 1920:2048].astype(F32) * gain).astype(BF)
-    gb_ref[5, :, 128:256] = (downw_ref[...].astype(F32) * gain).astype(BF)
-    gb_ref[5, :, 256:384] = jnp.zeros((64, 128), BF)
-    gb_ref[6:8] = jnp.zeros((2, 64, 384), BF)
+    for j in range(8):
+        gb_ref[j, :, 128:384] = (kvw_ref[:, j * 256:j * 256 + 256].astype(F32) * gain).astype(BF)
+    gb_ref[0, :, 0:128] = (downw_ref[...].astype(F32) * gain).astype(BF)
+    gb_ref[1:8, :, 0:128] = jnp.zeros((7, 64, 128), BF)
     copies0 = [
         pltpu.make_async_copy(x_ref, pad.at[3:7, 16:48], lsem.at[0]),
         pltpu.make_async_copy(w1_ref, wa.at[0], lsem.at[1]),
         pltpu.make_async_copy(w2_ref, wb.at[0], lsem.at[2]),
-        pltpu.make_async_copy(b1_ref, ba.at[0], lsem.at[3]),
+        pltpu.make_async_copy(own_b1, ba.at[0], lsem.at[3]),
         pltpu.make_async_copy(pt_ref, pb.at[0, :, 0:EXT], lsem.at[4]),
         pltpu.make_async_copy(gb_ref.at[pair], pb.at[0, :, EXT:2048], lsem.at[5]),
     ]
@@ -134,13 +132,33 @@
                 )
     fwd_copies = [push(pt_ref, pb.at[1, :, 0:EXT], other)]
     w_core = [
-        push(w1_ref, wa.at[1], other), push(w2_ref, wb.at[1], other), push(b1_ref, ba.at[1], other),
+        push(w1_ref, wa.at[1], other), push(w2_ref, wb.at[1], other), push(own_b1, ba.at[1], other),
     ]
-    w_y = [
-        push(w1_ref, wa.at[2], device(0, 1, 0, 0)),
-        push(w2_ref, wb.at[2], device(0, 3, 0, 0)),
-        push(b1_ref, ba.at[2], device(0, 1, 0, 0)),
-    ]
+    x_half = x % 2
+
+    def w1_rows(half, part_of, count):
+        return pl.ds(pl.multiple_of(half * 768 + part_of * 384, 16), count)
+
+    def w2_rows(half, part_of, count):
+        return pl.ds(pl.multiple_of(half * 192 + part_of * 96, 16), count)
+
+    w_y = []
+    for n in range(2):
+        rows1, rows2 = w1_rows(x_half, n, 384), w2_rows(x_half, n, 96)
+        w_y.append([
+            push(w1_ref.at[rows1], wa.at[2, rows1], device(0, 1, 0, 0)),
+            push(w2_ref.at[rows2], wb.at[2, rows2], device(0, 3, 0, 0)),
+        ])
+    w_y[0].append(push(own_b1, ba.at[2], device(0, 1, 0, 0)))
+
+    w_x = []
+
+    def share_w(n):
+        for copy in w_y[n]:
+            copy.wait()
+        rows1, rows2 = w1_rows(x_half, n, 384), w2_rows(x_half, n, 96)
+        w_x.append(push(wa.at[2, rows1], wa.at[2, rows1], device(1, 0, 0, 0)))
+        w_x.append(push(wb.at[2, rows2], wb.at[2, rows2], device(3, 0, 0, 0)))
 
     token = lax.broadcasted_iota(jnp.int32, (128, 128), 0)
     later = token >= 64
@@ -195,27 +213,147 @@
     for copy in fwd_copies:
         copy.wait()
 
-    def products(i, carry):
-        left = pb[:, :, pl.ds(pl.multiple_of(i * 128, 128), 128)].reshape(512, 128)
-        for t in range(3):
-            block = pair * 3 + t
-            shift = i + block - 17
-            around = jnp.where(shift >= 13, shift - 13, shift)
-            start = jnp.where(block < 17, 13 + t, around) * 128
-            right = pb[:, :, pl.ds(pl.multiple_of(start, 128), 128)].reshape(512, 128)
-            value = dot_tn(left, right).astype(BF).reshape(4, 2, 16, 128)
+    def products(quad, width, first):
+        def body(i, carry):
+            left = pb[:, :, pl.ds(pl.multiple_of(i * 128, 128), 128)].reshape(512, 128)
+            if first:
+                shift = i + pair - 1
+                around = jnp.where(shift >= 13, shift - 13, shift)
+                start = pl.multiple_of(jnp.where(pair == 0, 13, around) * 128, 128)
+            else:
+                start = EXT + 128
+            right = pb[:, :, pl.ds(start, width)].reshape(512, width)
+            value = dot_tn(left, right).astype(BF).reshape(4, 2, 16, width)
             for r in range(4):
                 p = i * 4 + r
-                quad[p // 12, p % 12, :, :, t * 128:t * 128 + 128] = value[r]
-        return carry
-
-    lax.fori_loop(0, 13, products, 0)
-    red_copies = []
-    for n, dz in enumerate((1, 3, 2)):
-        target = device(0, 0, dz, 0)
-        red_copies.append(push(quad.at[0:4, pl.ds(((z + dz) % 4) * 3, 3)], red_z.at[n], target))
-        red_copies.append(push(quad.at[4, 0, 0], red_bias.at[n], target))
-
+                quad[p // 12, p % 12] = value[r]
+            return carry
+
+        lax.fori_loop(0, 13, body, 0)
+
+    class Chain:
+        def __init__(self, quad, red_z, red_mid, red_y, red_bias, mf):
+            self.quad, self.red_z, self.red_mid = quad, red_z, red_mid
+            self.red_y, self.red_bias, self.mf = red_y, red_bias, mf
+
+        def start(self):
+            self.copies = []
+            for n, dz in enumerate((1, 3, 2)):
+                target = device(0, 0, dz, 0)
+                block = self.quad.at[0:4, pl.ds(((z + dz) % 4) * 3, 3)]
+                self.copies.append(push(block, self.red_z.at[n], target))
+                self.copies.append(push(self.quad.at[4, 0, 0], self.red_bias.at[n], target))
+
+        def middle(self):
+            for copy in self.copies:
+                copy.wait()
+
+            def body(n, carry):
+                h, p = n // 3, n % 3
+                total = self.quad[h, z * 3 + p].astype(F32)
+                for m in range(3):
+                    total = total + self.red_z[m, h, p].astype(F32)
+                self.red_mid[h, p] = total.astype(BF)
+                return carry
+
+            lax.fori_loop(0, 12, body, 0)
+            total = self.quad[4, 0, 0].astype(F32)
+            for m in range(3):
+                total = total + self.red_bias[m].astype(F32)
+            self.red_bias[6] = total.astype(BF)
+            self.copies = []
+            for n, dy in enumerate((1, 3, 2)):
+                target = device(0, dy, 0, 0)
+                self.copies.append(push(self.red_mid.at[(y + dy) % 4], self.red_y.at[n], target))
+                self.copies.append(push(self.red_bias.at[6], self.red_bias.at[3 + n], target))
+
+        def spread(self):
+            for copy in self.copies:
+                copy.wait()
+
+            def body(p, carry):
+                total = self.red_mid[y, p].astype(F32)
+                for m in range(3):
+                    total = total + self.red_y[m, p].astype(F32)
+                self.mf[pair, pl.ds(plane * 6 + p * 2, 2)] = total.astype(BF)
+                return carry
+
+            lax.fori_loop(0, 3, body, 0)
+            total = self.red_bias[6].astype(F32)
+            for m in range(3):
+                total = total + self.red_bias[3 + m].astype(F32)
+            self.mf[pair, 96] = total.astype(BF)
+            block = self.mf.at[pair, pl.ds(plane * 6, 6)]
+            self.copies = [push(block, block, device(0, 0, dz, 0)) for dz in (1, 3, 2)]
+
+        def fan(self):
+            for copy in self.copies:
+                copy.wait()
+            block = self.piece(pair, 0)
+            self.copies = [push(block, block, device(0, dy, 0, 0)) for dy in (1, 3, 2)]
+
+        def piece(self, owner, dy, low=0, count=24):
+            return self.mf.at[owner, pl.ds(((y + dy) % 4) * 24 + low, count)]
+
+    chain_a = Chain(quad_a, red_z_a, red_mid_a, red_y_a, red_bias_a, mf_a)
+    chain_b = Chain(quad_b, red_z_b, red_mid_b, red_y_b, red_bias_b, mf_b)
+    x_prev = ((x + 3) % 4) * 2 + core
+    x_next = ((x + 1) % 4) * 2 + core
+    x_far = ((x + 2) % 4) * 2 + core
+    m_core = []
+
+    def send_whole():
+        for copy in chain_a.copies:
+            copy.wait()
+        whole = mf_a.at[pair]
+        sent = [push(whole, whole, device(1, 0, 0, 0)), push(whole, whole, device(3, 0, 0, 0))]
+        m_core.append(push(whole, whole, other))
+        return sent
+
+    def relay_whole(sent):
+        sent[0].wait()
+        low, high = mf_a.at[x_prev, 0:48], mf_a.at[x_next, 48:97]
+        far = [push(low, low, device(1, 0, 0, 0))]
+        m_core.append(push(mf_a.at[x_prev], mf_a.at[x_prev], other))
+        sent[1].wait()
+        far.append(push(high, high, device(3, 0, 0, 0)))
+        m_core.append(push(mf_a.at[x_next], mf_a.at[x_next], other))
+        return far
+
+    def finish_whole(far):
+        for copy in far:
+            copy.wait()
+        push(mf_a.at[x_far], mf_a.at[x_far], other).wait()
+        for copy in m_core:
+            copy.wait()
+        del m_core[:]
+
+    piece = chain_b.piece
+
+    def send_piece(dy):
+        block = piece(pair, dy)
+        sent = [push(block, block, device(1, 0, 0, 0)), push(block, block, device(3, 0, 0, 0))]
+        m_core.append(push(block, block, other))
+        return sent
+
+    def relay_piece(dy, sent):
+        sent[0].wait()
+        low, high = piece(x_prev, dy, 0, 12), piece(x_next, dy, 12, 12)
+        far = [push(low, low, device(1, 0, 0, 0))]
+        m_core.append(push(piece(x_prev, dy), piece(x_prev, dy), other))
+        sent[1].wait()
+        far.append(push(high, high, device(3, 0, 0, 0)))
+        m_core.append(push(piece(x_next, dy), piece(x_next, dy), other))
+        return far
+
+    def finish_piece(dy, far):
+        far[0].wait()
+        far[1].wait()
+        m_core.append(push(piece(x_far, dy), piece(x_far, dy), other))
+
+    products(quad_a, 128, True)
+    chain_a.start()
+    share_w(0)
     h_rt.wait()
     h_lt.wait()
     for copy in corners:
@@ -231,7 +369,7 @@
 
     def conv_lanes(n, carry):
         lanes = pl.ds(pl.multiple_of(n * 128, 128), 128)
-        sums = [jnp.zeros((32, 128), F32) + dbias_ref[0:1, lanes] for _ in range(4)]
+        sums = [jnp.zeros((32, 128), F32) + dbias_ref[lanes].reshape(1, 128) for _ in range(4)]
         for wp in range(10):
             full = pad[wp, :, lanes].astype(F32)
             moved = pltpu.roll(full, 60, 0)
@@ -253,7 +391,7 @@
         center = jnp.sum(value, axis=-1, keepdims=True) * (1.0 / CHANNELS)
         centered = value - center
         variance = jnp.sum(centered * centered, axis=-1, keepdims=True) * (1.0 / CHANNELS)
-        value = centered * lax.rsqrt(variance + 1e-06) * lgain_ref[...] + lshift_ref[...]
+        value = centered * lax.rsqrt(variance + 1e-06) * lgain_ref[...].reshape(1, CHANNELS) + lshift_ref[...].reshape(1, CHANNELS)
         part[0, w, rows, :] = value.astype(BF)
         return carry
 
@@ -264,6 +402,10 @@
     t_next = push(tok.at[0], tok.at[1], device(0, 0, 1, 0))
     t_prev = push(tok.at[0], tok.at[2], device(0, 0, 3, 0))
 
+    share_w(1)
+    products(quad_b, 256, False)
+    chain_b.start()
+    chain_a.middle()
     def mlp(slot, count, weights, first):
         rows = 128 * count
         tokens = tok[slot:slot + count].reshape(rows, CHANNELS)
@@ -288,120 +430,46 @@
             )
         return sent
 
-    scale = scale_ref[...]
+    scale = scale_ref[...].reshape(1, CHANNELS)
     mlp(0, 1, (0,), True)
     for copy in w_core:
         copy.wait()
     mlp(0, 1, (1,), False)
 
-    for copy in red_copies:
-        copy.wait()
-
-    def sum_z(n, carry):
-        h, p = n // 3, n % 3
-        total = quad[h, z * 3 + p].astype(F32)
-        for m in range(3):
-            total = total + red_z[m, h, p].astype(F32)
-        red_mid[h, p] = total.astype(BF)
-        return carry
-
-    lax.fori_loop(0, 12, sum_z, 0)
-    total = quad[4, 0, 0].astype(F32)
-    for m in range(3):
-        total = total + red_bias[m].astype(F32)
-    red_bias[6] = total.astype(BF)
-    red_copies = []
-    for n, dy in enumerate((1, 3, 2)):
-        target = device(0, dy, 0, 0)
-        red_copies.append(push(red_mid.at[(y + dy) % 4], red_y.at[n], target))
-        red_copies.append(push(red_bias.at[6], red_bias.at[3 + n], target))
+    chain_a.spread()
+    own_half = [(wa, w1_rows(x_half, 0, 768)), (wb, w2_rows(x_half, 0, 192))]
+    their_half = [(wa, w1_rows(1 - x_half, 0, 768)), (wb, w2_rows(1 - x_half, 0, 192))]
+    w_fwd = [push(ref.at[2, rows], ref.at[3, rows], other) for ref, rows in own_half]
+    w_fwd.append(push(ba.at[2], ba.at[3], other))
     t_next.wait()
     t_far0 = push(tok.at[1, 0:64], tok.at[3, 0:64], device(0, 0, 1, 0))
     t_prev.wait()
     t_far1 = push(tok.at[2, 64:128], tok.at[3, 64:128], device(0, 0, 3, 0))
-    for copy in red_copies:
-        copy.wait()
-
-    def sum_y(p, carry):
-        total = red_mid[y, p].astype(F32)
-        for m in range(3):
-            total = total + red_y[m, p].astype(F32)
-        mf[pair, pl.ds(plane * 6 + p * 2, 2)] = total.astype(BF)
-        return carry
-
-    lax.fori_loop(0, 3, sum_y, 0)
-    total = red_bias[6].astype(F32)
-    for m in range(3):
-        total = total + red_bias[3 + m].astype(F32)
-    mf[pair, 96] = total.astype(BF)
-    block = mf.at[pair, pl.ds(plane * 6, 6)]
-    all_z = [push(block, block, device(0, 0, dz, 0)) for dz in (1, 3, 2)]
-    m_bias = [push(mf.at[pair, 96], mf.at[pair, 96], device(dx, 0, 0, 0)) for dx in (1, 3, 2)]
-    for copy in w_y:
-        copy.wait()
-    w_fwd = [
-        push(wa.at[2], wa.at[3], other), push(wb.at[2], wb.at[3], other), push(ba.at[2], ba.at[3], other),
-    ]
+    for copy in w_x:
+        copy.wait()
+    w_fwd += [push(ref.at[2, rows], ref.at[3, rows], other) for ref, rows in their_half]
     mlp(0, 1, (2,), False)
     for copy in w_fwd:
         copy.wait()
     mlp(0, 1, (3,), False)
-    part[0] = (acc[0:128, :] * scale + (feat[...] + scale * rbias_ref[...])).astype(BF).reshape(4, 32, CHANNELS)
+    part[0] = (acc[0:128, :] * scale + (feat[...] + scale * rbias_ref[...].reshape(1, CHANNELS))).astype(BF).reshape(4, 32, CHANNELS)
     scatters = scatter(0)
-
-    x_prev = ((x + 3) % 4) * 2 + core
-    x_next = ((x + 1) % 4) * 2 + core
-    x_far = ((x + 2) % 4) * 2 + core
-
-    def piece(owner, dy, low=0, count=24):
-        return mf.at[owner, pl.ds(((y + dy) % 4) * 24 + low, count)]
-
-    m_core = []
-
-    def send_piece(dy):
-        sent = [
-            push(piece(pair, dy), piece(pair, dy), device(1, 0, 0, 0)),
-            push(piece(pair, dy), piece(pair, dy), device(3, 0, 0, 0)),
-        ]
-        m_core.append(push(piece(pair, dy), piece(pair, dy), other))
-        return sent
-
-    def relay_piece(dy, sent):
-        sent[0].wait()
-        far = [push(piece(x_prev, dy, 0, 12), piece(x_prev, dy, 0, 12), device(1, 0, 0, 0))]
-        m_core.append(push(piece(x_prev, dy), piece(x_prev, dy), other))
-        sent[1].wait()
-        far.append(push(piece(x_next, dy, 12, 12), piece(x_next, dy, 12, 12), device(3, 0, 0, 0)))
-        m_core.append(push(piece(x_next, dy), piece(x_next, dy), other))
-        return far
-
-    def finish_piece(dy, far):
-        far[0].wait()
-        far[1].wait()
-        m_core.append(push(piece(x_far, dy), piece(x_far, dy), other))
-
-    for copy in all_z:
-        copy.wait()
-    all_y = [push(piece(pair, 0), piece(pair, 0), device(0, dy, 0, 0)) for dy in (1, 3, 2)]
-    sent_0 = send_piece(0)
+    chain_a.fan()
     mlp(1, 2, (0, 1, 2, 3), True)
     for slot in (1, 2):
         part[slot] = (acc[128 * slot - 128:128 * slot, :] * scale).astype(BF).reshape(4, 32, CHANNELS)
         scatters += scatter(slot)
-    all_y[0].wait()
-    sent_3 = send_piece(3)
-    far_0 = relay_piece(0, sent_0)
+    sent_a = send_whole()
+    chain_b.middle()
     t_far0.wait()
     t_far1.wait()
     mlp(3, 1, (0, 1, 2, 3), True)
     part[3] = (acc[0:128, :] * scale).astype(BF).reshape(4, 32, CHANNELS)
     scatters += scatter(3)
-    all_y[1].wait()
-    sent_1 = send_piece(1)
-    all_y[2].wait()
-    sent_2 = send_piece(2)
-    finish_piece(0, far_0)
-    far_3 = relay_piece(3, sent_3)
+    chain_b.spread()
+    far_a = relay_whole(sent_a)
+    chain_b.fan()
+    b_bias = [push(mf_b.at[pair, 96], mf_b.at[pair, 96], device(dx, 0, 0, 0)) for dx in (1, 3, 2)]
     for copy in scatters:
         copy.wait()
 
@@ -424,6 +492,7 @@
                 seq_copies.append(push(stage_b.at[q], seq_in.at[my_q], device(0, dy * yflip, 0, dk)))
     seq_in[my_q] = stage_b[my_q]
 
+    sent_0 = send_piece(0)
     for copy in seq_copies:
         copy.wait()
     for n in range(3):
@@ -437,56 +506,29 @@
         else:
             lanes = slice((b % 13) * 128, (b % 13) * 128 + 128)
             ext[:, b * 128:b * 128 + 128] = tok[0, :, lanes].astype(F32)
-    far_1 = relay_piece(1, sent_1)
-    finish_piece(3, far_3)
-    far_2 = relay_piece(2, sent_2)
-    finish_piece(1, far_1)
-    for copy in m_bias:
-        copy.wait()
-    for owner in (pair, x_prev, x_next, x_far):
-        m_core.append(push(mf.at[owner, 96], mf.at[owner, 96], other))
-    finish_piece(2, far_2)
-    for copy in m_core:
-        copy.wait()
+    finish_whole(far_a)
+    all_y = chain_b.copies
+    all_y[0].wait()
+    sent_3 = send_piece(3)
 
     encoded = tok[0]
 
     def squares_of(i, total):
         cells = tok[0, :, pl.ds(pl.multiple_of(i * 128, 128), 128)]
-        groups = pl.ds(i * 8, 8)
-
-        def other_block(d):
-            return ext[:, pl.ds(pl.multiple_of((i + d) * 128, 128), 128)]
-
-        total = total + dot(cells, mf[5, groups, :, 256:384].reshape(128, 128)) * other_block(0)
-        for j in (6, 7):
-            value = 2.0 * dot(cells, mf[j, groups].reshape(128, 384))
-            for t in range(3):
-                total = total + value[:, t * 128:t * 128 + 128] * other_block((j - 6) * 3 + t + 1)
+        for d in range(7):
+            value = dot(cells, mf_a[1 + d, pl.ds(i * 8, 8)].reshape(128, 128))
+            turned = ext[:, pl.ds(pl.multiple_of((i + d) * 128, 128), 128)]
+            total = total + (1.0 if d == 0 else 2.0) * (value * turned)
         return total
 
     total = lax.fori_loop(0, BLOCKS, squares_of, jnp.zeros((128, 128), F32))
     for d in range(7):
-        j, t = (17 + d) // 3, (17 + d) % 3
-        weight = mf[j, 96, :, t * 128:t * 128 + 128].astype(F32)[0:1]
+        weight = mf_a[1 + d, 96].astype(F32)[0:1]
         total = total + (1.0 if d == 0 else 2.0) * weight * ext[:, (12 + d) * 128:(13 + d) * 128]
     squares = jnp.maximum(jnp.sum(total, axis=-1, keepdims=True), 0.0)
     inverse = lax.rsqrt(squares * (1.0 / LANGUAGE_WIDTH) + 1e-06)
-    for j in range(6):
-        offset = mf[j, 96].astype(F32)[0:1]
-        lin[:, j * 384:j * 384 + 384] = inverse * (dot(encoded, mf[j, 0:96].reshape(CHANNELS, 384)) + offset)
-    adapter_in = lin[:, 2048:2176].astype(BF)
-    for n in range(8):
-        lanes = slice(n * 256, n * 256 + 256)
-        value = lin[:, lanes] + kvb_ref[0:1, lanes] + dot(adapter_in, up_ref[:, lanes])
-        if n < 4:
-            for h in range(2):
-                head = value[:, h * 128:h * 128 + 128]
-                turned = head * cosine + pltpu.roll(head, 64, 1) * sine
-                kv_ref[:, n * 256 + h * 128:n * 256 + h * 128 + 128] = turned.astype(BF)
-        else:
-            kv_ref[:, lanes] = value.astype(BF)
-
+    adapter_in = dot(encoded, mf_a[0, 0:96].reshape(CHANNELS, 128)) + mf_a[0, 96].astype(F32)[0:1]
+    adapter_in = (inverse * adapter_in).astype(BF)
     weighted = (inverse * adapter_grad).astype(BF)
 
     def place(group, value):
@@ -507,7 +549,12 @@
     for half in range(2):
         for p in range(16):
             ein[half, p, 5] = shifted
-    push(ein.at[1 - core], e_core, other).wait()
+    joined = push(ein.at[1 - core], e_core, other)
+    all_y[1].wait()
+    sent_1 = send_piece(1)
+    all_y[2].wait()
+    sent_2 = send_piece(2)
+    joined.wait()
 
     def sum_cores(p, carry):
         e_mid[p] = (ein[core, p].astype(F32) + e_core[p].astype(F32)).astype(BF)
@@ -518,6 +565,8 @@
     for n, (dy, dz) in enumerate(planes):
         target_plane = ((y + dy) % 4) * 4 + (z + dz) % 4
         sums.append(push(e_mid.at[target_plane], e_in1.at[n], device(0, dy, dz, 0)))
+    far_0 = relay_piece(0, sent_0)
+    far_3 = relay_piece(3, sent_3)
     for copy in sums:
         copy.wait()
     value = e_mid[plane].astype(F32)
@@ -525,6 +574,8 @@
         value = value + e_in1[n].astype(F32)
     e_in2[x] = value.astype(BF)
     sums = [push(e_in2.at[x], e_in2.at[x], device(dx, 0, 0, 0)) for dx in (1, 3, 2)]
+    far_1 = relay_piece(1, sent_1)
+    finish_piece(0, far_0)
     for copy in sums:
         copy.wait()
     value = e_in2[0].astype(F32)
@@ -533,12 +584,35 @@
     value = value.astype(BF)
     mine = e_all.at[pl.ds(core * 80 + plane * 5, 5)]
     mine[...] = value[0:5]
+    total_shift = value[5].astype(F32)[0:1]
     sums = [push(mine, mine, device(0, dy, dz, 0)) for dy, dz in planes]
+    far_2 = relay_piece(2, sent_2)
+    finish_piece(3, far_3)
+    finish_piece(1, far_1)
+    for copy in b_bias:
+        copy.wait()
+    for owner in (pair, x_prev, x_next, x_far):
+        m_core.append(push(mf_b.at[owner, 96], mf_b.at[owner, 96], other))
+    finish_piece(2, far_2)
     for copy in sums:
         copy.wait()
     mine = e_all.at[pl.ds(core * 80, 80)]
-    push(mine, mine, other).wait()
-    total_shift = value[5].astype(F32)[0:1]
+    joined = push(mine, mine, other)
+    for copy in m_core:
+        copy.wait()
+
+    for n in range(8):
+        lanes = slice(n * 256, n * 256 + 256)
+        value = dot(encoded, mf_b[n, 0:96].reshape(CHANNELS, 256)) + mf_b[n, 96].astype(F32)[0:1]
+        value = inverse * value + (kvb_ref[0:1, lanes] + dot(adapter_in, up_ref[:, lanes]))
+        if n < 4:
+            for h in range(2):
+                head = value[:, h * 128:h * 128 + 128]
+                turned = head * cosine + pltpu.roll(head, 64, 1) * sine
+                kv_ref[:, n * 256 + h * 128:n * 256 + h * 128 + 128] = turned.astype(BF)
+        else:
+            kv_ref[:, lanes] = value.astype(BF)
+    joined.wait()
     down = dot(pt_ref[:, 0:CHANNELS], e_all[0:96].reshape(CHANNELS, 128))
     down_ref[...] = (down + bias * total_shift) * gain
     for n in range(16):
@@ -581,7 +655,7 @@
             jax.ShapeDtypeStruct((64, 128), F32),
             jax.ShapeDtypeStruct((2, 64, 1024), F32),
         ),
-        in_specs=[vmem] * 17 + [pl.BlockSpec(memory_space=pltpu.SMEM)] + [vmem] * 4,
+        in_specs=[vmem] * 5 + [pl.BlockSpec(memory_space=pl.ANY)] * 2 + [vmem] * 10 + [pl.BlockSpec(memory_space=pltpu.SMEM)] + [vmem] * 4,
         out_specs=(vmem, vmem, vmem),
         scratch_shapes=[
             pltpu.VMEM((10, 64, CHANNELS), BF),
@@ -598,14 +672,19 @@
             pltpu.VMEM((4, 32, CHANNELS), BF),
             pltpu.VMEM((4, 32, CHANNELS), BF),
             pltpu.VMEM((8, 64, 2048), BF),
-            pltpu.VMEM((5, 12, 2, 16, 384), BF),
-            pltpu.VMEM((3, 4, 3, 2, 16, 384), BF),
-            pltpu.VMEM((4, 3, 2, 16, 384), BF),
-            pltpu.VMEM((3, 3, 2, 16, 384), BF),
-            pltpu.VMEM((7, 16, 384), BF),
-            pltpu.VMEM((8, 97, 16, 384), BF),
+            pltpu.VMEM((5, 12, 2, 16, 128), BF),
+            pltpu.VMEM((3, 4, 3, 2, 16, 128), BF),
+            pltpu.VMEM((4, 3, 2, 16, 128), BF),
+            pltpu.VMEM((3, 3, 2, 16, 128), BF),
+            pltpu.VMEM((7, 16, 128), BF),
+            pltpu.VMEM((8, 97, 16, 128), BF),
+            pltpu.VMEM((5, 12, 2, 16, 256), BF),
+            pltpu.VMEM((3, 4, 3, 2, 16, 256), BF),
+            pltpu.VMEM((4, 3, 2, 16, 256), BF),
+            pltpu.VMEM((3, 3, 2, 16, 256), BF),
+            pltpu.VMEM((7, 16, 256), BF),
+            pltpu.VMEM((8, 97, 16, 256), BF),
             pltpu.VMEM((128, 19 * 128), F32),
-            pltpu.VMEM((128, 2304), F32),
             pltpu.VMEM((128, 2048), BF),
             pltpu.VMEM((2, 16, 6, 16, 128), BF),
             pltpu.VMEM((16, 6, 16, 128), BF),
@@ -619,6 +698,7 @@
             pltpu.VMEM((7, 8, CHANNELS), F32),
             pltpu.VMEM((128, 128), F32),
             pltpu.VMEM((128, 128), F32),
+            pltpu.VMEM((1, 384), F32),
             pltpu.SemaphoreType.DMA((COPIES,)),
             pltpu.SemaphoreType.DMA((COPIES,)),
             pltpu.SemaphoreType.DMA((6,)),
@@ -628,9 +708,9 @@
         ),
         cost_estimate=pl.CostEstimate(flops=8_000_000_000, bytes_accessed=30_000_000, transcendentals=0),
     )(
-        cells, depthwise_kernel, depthwise_bias[None, :], layer_norm_gain[None, :], layer_norm_shift[None, :],
-        expansion_weight, reduction_weight, expansion_bias[None, :], reduction_bias[None, :],
-        layer_branch_scale[None, :], projector_weight, projector_bias[None, :], input_norm_gain[None, :],
+        cells, depthwise_kernel, depthwise_bias, layer_norm_gain, layer_norm_shift,
+        expansion_weight, reduction_weight, expansion_bias, reduction_bias,
+        layer_branch_scale, projector_weight.T, projector_bias[None, :], input_norm_gain[None, :],
         key_value_weight, key_value_bias[None, :], adapter_down_weight, adapter_up_weight,
         image_start_positions, key_value_cotangent.reshape(128, 2048), freq, tile_order, seq_order,
     )

time: 166 us -> 143 us (0.86)
  Pallas kernels: 149 us -> 137 us
  local copies, waits for them, and re-layouts: 15.5 us -> 5.92 us
    pallas_call x1, Pallas kernels: 149 us -> 137 us  [local(): pl.pallas_call(kernel, out_shape=(jax.ShapeDtypeStruct((128, 2048), BF),...]
    broadcast_in_dim x6 -> x0, local copies, waits for them, and re-layouts: 7.72 us -> none  [the longest x1 1.3 us: local(): layer_norm_shift[None, :]]
    unnamed x6 -> x5, local copies, waits for them, and re-layouts: 5.96 us -> 4.11 us
where the time goes in v4:
time: 143 us
  Pallas kernels  137 us (96%)
  local copies, waits for them, and re-layouts  5.92 us (4%)
    pallas_call x1, Pallas kernels, local(): pl.pallas_call(kernel, out_shape=(jax.ShapeDtypeStruct((128, 2048), BF),...  137 us
    unnamed x5, local copies, waits for them, and re-layouts  4.11 us

profile of v4, /device:TPU:1, one launch (start us, length us, event | category | flops | bytes accessed | tf_op | source)
XLA Modules:
  0.0 143.1 jit_solution(16974464736203656274)
XLA Ops:
  0.6 1.8 %copy.26.x_ref = bf16[4,32,1536]{2,1,0:T(8,128)(2,1)} copy(bf16[4,32,1536]{2,0,1:T(4,128)(2,1)} %bitcast.10) | data formatting | bytes 786432 | tf_op jit(solution)/shard_map/reshape | solution.py:646
  2.4 136.5 %shard_map.229 = (bf16[128,2048]{1,0:T(8,128)(2,1)}, f32[64,128]{1,0:T(8,128)}, f32[2,64,1024]{2,1,0:T(8,128)}) custom-call(bf16[4,32,1536]{2,1,0:T(8,128)(2,1)} %copy.26.x_ref, bf16[7,7,1536]{2,1,0:T(8,128)(2,1)} %depth_ref.1, f32[1536]{0:T(1024)} %dbias_ref.1, f32[1536]{0:T(1024)} %lgain_ref.1, f32[1536]{0:T(1024)} %lshift_ref.1, ...), custom_call_target="tpu_custom_call" | custom-call | flops 8000000000 | bytes 30000000 | tf_op jit(solution)/shard_map/pallas_call | solution.py:651
  139.0 0.0 copy-start
  139.0 1.9 %copy.30 = bf16[2,64,2048]{2,1,0:T(8,128)(2,1)} copy(bf16[2,64,2048]{2,1,0:T(8,128)(2,1)} %bitcast.9) | data formatting | bytes 1048576
  140.9 1.4 copy.31
  142.3 0.0 copy-done
  142.3 0.8 copy.32
Async XLA Ops:
  139.0 3.3 %copy-start = (f32[2,64,1024]{2,1,0:T(8,128)S(1)}, f32[2,64,1024]{2,1,0:T(8,128)}, u32[]{:S(2)}) copy-start(f32[2,64,1024]{2,1,0:T(8,128)} %get-tuple-element.14) | copy-start | bytes 1572868

commit v5 on v4

--- a/solution.py
+++ b/solution.py
@@ -232,16 +232,24 @@
         lax.fori_loop(0, 13, body, 0)
 
     class Chain:
-        def __init__(self, quad, red_z, red_mid, red_y, red_bias, mf):
-            self.quad, self.red_z, self.red_mid = quad, red_z, red_mid
-            self.red_y, self.red_bias, self.mf = red_y, red_bias, mf
+        def __init__(self, first, quad, red_1, red_mid, red_2, red_bias, mf):
+            self.quad, self.red_1, self.red_mid = quad, red_1, red_mid
+            self.red_2, self.red_bias, self.mf = red_2, red_bias, mf
+            self.first = first
+            self.third = lambda n: pl.ds(((z + n) % 4) * 3, 3)
+
+        def toward(self, axis, n):
+            return device(0, n, 0, 0) if axis == 1 else device(0, 0, n, 0)
 
         def start(self):
             self.copies = []
-            for n, dz in enumerate((1, 3, 2)):
-                target = device(0, 0, dz, 0)
-                block = self.quad.at[0:4, pl.ds(((z + dz) % 4) * 3, 3)]
-                self.copies.append(push(block, self.red_z.at[n], target))
+            for n, step in enumerate((1, 3, 2)):
+                target = self.toward(self.first, step)
+                if self.first == 2:
+                    block = self.quad.at[0:4, self.third(step)]
+                else:
+                    block = self.quad.at[(y + step) % 4]
+                self.copies.append(push(block, self.red_1.at[n], target))
                 self.copies.append(push(self.quad.at[4, 0, 0], self.red_bias.at[n], target))
 
         def middle(self):
@@ -249,11 +257,14 @@
                 copy.wait()
 
             def body(n, carry):
-                h, p = n // 3, n % 3
-                total = self.quad[h, z * 3 + p].astype(F32)
+                if self.first == 2:
+                    own, place = (n // 3, z * 3 + n % 3), (n // 3, n % 3)
+                else:
+                    own, place = (y, n), (n,)
+                total = self.quad[own].astype(F32)
                 for m in range(3):
-                    total = total + self.red_z[m, h, p].astype(F32)
-                self.red_mid[h, p] = total.astype(BF)
+                    total = total + self.red_1[(m,) + place].astype(F32)
+                self.red_mid[place] = total.astype(BF)
                 return carry
 
             lax.fori_loop(0, 12, body, 0)
@@ -262,9 +273,13 @@
                 total = total + self.red_bias[m].astype(F32)
             self.red_bias[6] = total.astype(BF)
             self.copies = []
-            for n, dy in enumerate((1, 3, 2)):
-                target = device(0, dy, 0, 0)
-                self.copies.append(push(self.red_mid.at[(y + dy) % 4], self.red_y.at[n], target))
+            for n, step in enumerate((1, 3, 2)):
+                target = self.toward(3 - self.first, step)
+                if self.first == 2:
+                    block = self.red_mid.at[(y + step) % 4]
+                else:
+                    block = self.red_mid.at[self.third(step)]
+                self.copies.append(push(block, self.red_2.at[n], target))
                 self.copies.append(push(self.red_bias.at[6], self.red_bias.at[3 + n], target))
 
         def spread(self):
@@ -272,9 +287,10 @@
                 copy.wait()
 
             def body(p, carry):
-                total = self.red_mid[y, p].astype(F32)
+                own = (y, p) if self.first == 2 else (z * 3 + p,)
+                total = self.red_mid[own].astype(F32)
                 for m in range(3):
-                    total = total + self.red_y[m, p].astype(F32)
+                    total = total + self.red_2[m, p].astype(F32)
                 self.mf[pair, pl.ds(plane * 6 + p * 2, 2)] = total.astype(BF)
                 return carry
 
@@ -295,8 +311,8 @@
         def piece(self, owner, dy, low=0, count=24):
             return self.mf.at[owner, pl.ds(((y + dy) % 4) * 24 + low, count)]
 
-    chain_a = Chain(quad_a, red_z_a, red_mid_a, red_y_a, red_bias_a, mf_a)
-    chain_b = Chain(quad_b, red_z_b, red_mid_b, red_y_b, red_bias_b, mf_b)
+    chain_a = Chain(2, quad_a, red_z_a, red_mid_a, red_y_a, red_bias_a, mf_a)
+    chain_b = Chain(1, quad_b, red_z_b, red_mid_b, red_y_b, red_bias_b, mf_b)
     x_prev = ((x + 3) % 4) * 2 + core
     x_next = ((x + 1) % 4) * 2 + core
     x_far = ((x + 2) % 4) * 2 + core
@@ -441,6 +457,7 @@
     their_half = [(wa, w1_rows(1 - x_half, 0, 768)), (wb, w2_rows(1 - x_half, 0, 192))]
     w_fwd = [push(ref.at[2, rows], ref.at[3, rows], other) for ref, rows in own_half]
     w_fwd.append(push(ba.at[2], ba.at[3], other))
+    chain_a.fan()
     t_next.wait()
     t_far0 = push(tok.at[1, 0:64], tok.at[3, 0:64], device(0, 0, 1, 0))
     t_prev.wait()
@@ -449,27 +466,32 @@
         copy.wait()
     w_fwd += [push(ref.at[2, rows], ref.at[3, rows], other) for ref, rows in their_half]
     mlp(0, 1, (2,), False)
+    chain_b.middle()
     for copy in w_fwd:
         copy.wait()
     mlp(0, 1, (3,), False)
     part[0] = (acc[0:128, :] * scale + (feat[...] + scale * rbias_ref[...].reshape(1, CHANNELS))).astype(BF).reshape(4, 32, CHANNELS)
     scatters = scatter(0)
-    chain_a.fan()
+    sent_a = send_whole()
+    chain_b.spread()
     mlp(1, 2, (0, 1, 2, 3), True)
     for slot in (1, 2):
         part[slot] = (acc[128 * slot - 128:128 * slot, :] * scale).astype(BF).reshape(4, 32, CHANNELS)
         scatters += scatter(slot)
-    sent_a = send_whole()
-    chain_b.middle()
+    chain_b.fan()
+    b_bias = [push(mf_b.at[pair, 96], mf_b.at[pair, 96], device(dx, 0, 0, 0)) for dx in (1, 3, 2)]
     t_far0.wait()
     t_far1.wait()
     mlp(3, 1, (0, 1, 2, 3), True)
     part[3] = (acc[0:128, :] * scale).astype(BF).reshape(4, 32, CHANNELS)
     scatters += scatter(3)
-    chain_b.spread()
     far_a = relay_whole(sent_a)
-    chain_b.fan()
-    b_bias = [push(mf_b.at[pair, 96], mf_b.at[pair, 96], device(dx, 0, 0, 0)) for dx in (1, 3, 2)]
+    sent_0 = send_piece(0)
+    all_y = chain_b.copies
+    all_y[0].wait()
+    sent_3 = send_piece(3)
+    all_y[1].wait()
+    sent_1 = send_piece(1)
     for copy in scatters:
         copy.wait()
 
@@ -492,7 +514,9 @@
                 seq_copies.append(push(stage_b.at[q], seq_in.at[my_q], device(0, dy * yflip, 0, dk)))
     seq_in[my_q] = stage_b[my_q]
 
-    sent_0 = send_piece(0)
+    all_y[2].wait()
+    sent_2 = send_piece(2)
+    far_0 = relay_piece(0, sent_0)
     for copy in seq_copies:
         copy.wait()
     for n in range(3):
@@ -507,9 +531,6 @@
             lanes = slice((b % 13) * 128, (b % 13) * 128 + 128)
             ext[:, b * 128:b * 128 + 128] = tok[0, :, lanes].astype(F32)
     finish_whole(far_a)
-    all_y = chain_b.copies
-    all_y[0].wait()
-    sent_3 = send_piece(3)
 
     encoded = tok[0]
 
@@ -550,10 +571,7 @@
         for p in range(16):
             ein[half, p, 5] = shifted
     joined = push(ein.at[1 - core], e_core, other)
-    all_y[1].wait()
-    sent_1 = send_piece(1)
-    all_y[2].wait()
-    sent_2 = send_piece(2)
+    far_3 = relay_piece(3, sent_3)
     joined.wait()
 
     def sum_cores(p, carry):
@@ -565,8 +583,8 @@
     for n, (dy, dz) in enumerate(planes):
         target_plane = ((y + dy) % 4) * 4 + (z + dz) % 4
         sums.append(push(e_mid.at[target_plane], e_in1.at[n], device(0, dy, dz, 0)))
-    far_0 = relay_piece(0, sent_0)
-    far_3 = relay_piece(3, sent_3)
+    far_1 = relay_piece(1, sent_1)
+    finish_piece(0, far_0)
     for copy in sums:
         copy.wait()
     value = e_mid[plane].astype(F32)
@@ -574,8 +592,8 @@
         value = value + e_in1[n].astype(F32)
     e_in2[x] = value.astype(BF)
     sums = [push(e_in2.at[x], e_in2.at[x], device(dx, 0, 0, 0)) for dx in (1, 3, 2)]
-    far_1 = relay_piece(1, sent_1)
-    finish_piece(0, far_0)
+    far_2 = relay_piece(2, sent_2)
+    finish_piece(3, far_3)
     for copy in sums:
         copy.wait()
     value = e_in2[0].astype(F32)
@@ -586,8 +604,6 @@
     mine[...] = value[0:5]
     total_shift = value[5].astype(F32)[0:1]
     sums = [push(mine, mine, device(0, dy, dz, 0)) for dy, dz in planes]
-    far_2 = relay_piece(2, sent_2)
-    finish_piece(3, far_3)
     finish_piece(1, far_1)
     for copy in b_bias:
         copy.wait()
@@ -679,8 +695,8 @@
             pltpu.VMEM((7, 16, 128), BF),
             pltpu.VMEM((8, 97, 16, 128), BF),
             pltpu.VMEM((5, 12, 2, 16, 256), BF),
-            pltpu.VMEM((3, 4, 3, 2, 16, 256), BF),
-            pltpu.VMEM((4, 3, 2, 16, 256), BF),
+            pltpu.VMEM((3, 12, 2, 16, 256), BF),
+            pltpu.VMEM((12, 2, 16, 256), BF),
             pltpu.VMEM((3, 3, 2, 16, 256), BF),
             pltpu.VMEM((7, 16, 256), BF),
             pltpu.VMEM((8, 97, 16, 256), BF),

time: 143 us -> 134 us (0.937)
  Pallas kernels: 137 us -> 127 us
    pallas_call x1, Pallas kernels: 137 us -> 127 us  [local(): pl.pallas_call(kernel, out_shape=(jax.ShapeDtypeStruct((128, 2048), BF),...]
where the time goes in v5:
time: 134 us
  Pallas kernels  127 us (95%)
  local copies, waits for them, and re-layouts  5.92 us (4%)
    pallas_call x1, Pallas kernels, local(): pl.pallas_call(kernel, out_shape=(jax.ShapeDtypeStruct((128, 2048), BF),...  127 us
    unnamed x5, local copies, waits for them, and re-layouts  4.11 us

profile of v5, /device:TPU:1, one launch (start us, length us, event | category | flops | bytes accessed | tf_op | source)
XLA Modules:
  0.0 133.8 jit_solution(6087329863179900560)
XLA Ops:
  0.6 1.8 %copy.26.x_ref = bf16[4,32,1536]{2,1,0:T(8,128)(2,1)} copy(bf16[4,32,1536]{2,0,1:T(4,128)(2,1)} %bitcast.10) | data formatting | bytes 786432 | tf_op jit(solution)/shard_map/reshape | solution.py:662
  2.4 127.2 %shard_map.229 = (bf16[128,2048]{1,0:T(8,128)(2,1)}, f32[64,128]{1,0:T(8,128)}, f32[2,64,1024]{2,1,0:T(8,128)}) custom-call(bf16[4,32,1536]{2,1,0:T(8,128)(2,1)} %copy.26.x_ref, bf16[7,7,1536]{2,1,0:T(8,128)(2,1)} %depth_ref.1, f32[1536]{0:T(1024)} %dbias_ref.1, f32[1536]{0:T(1024)} %lgain_ref.1, f32[1536]{0:T(1024)} %lshift_ref.1, ...), custom_call_target="tpu_custom_call" | custom-call | flops 8000000000 | bytes 30000000 | tf_op jit(solution)/shard_map/pallas_call | solution.py:667
  129.7 0.0 copy-start
  129.7 1.9 %copy.30 = bf16[2,64,2048]{2,1,0:T(8,128)(2,1)} copy(bf16[2,64,2048]{2,1,0:T(8,128)(2,1)} %bitcast.9) | data formatting | bytes 1048576
  131.6 1.4 %copy.31 = f32[64,128]{1,0:T(8,128)} copy(f32[64,128]{1,0:T(8,128)} %get-tuple-element.13) | data formatting | bytes 65536
  133.0 0.0 copy-done
  133.0 0.8 copy.32
Async XLA Ops:
  129.7 3.3 %copy-start = (f32[2,64,1024]{2,1,0:T(8,128)S(1)}, f32[2,64,1024]{2,1,0:T(8,128)}, u32[]{:S(2)}) copy-start(f32[2,64,1024]{2,1,0:T(8,128)} %get-tuple-element.14) | copy-start | bytes 1572868

commit v6 on v5

--- a/solution.py
+++ b/solution.py
@@ -37,16 +37,41 @@
 
 
 def kernel(
-    x_ref, depth_ref, dbias_ref, lgain_ref, lshift_ref, w1_ref, w2_ref, b1_ref, rbias_ref, scale_ref,
-    proj_ref, pbias_ref, ngain_ref, kvw_ref, kvb_ref, downw_ref, upw_ref, start_ref, cot_ref,
-    freq_ref, perm_ref, seq_ref,
-    kv_ref, down_ref, upg_ref,
+    x_hbm, depth_hbm, dbias_hbm, lgain_hbm, lshift_hbm, w1_hbm, w2_hbm, b1_hbm, rbias_hbm, scale_hbm, proj_hbm, pbias_hbm, ngain_hbm, kvw_hbm, kvb_hbm, downw_hbm, upw_hbm, start_ref, cot_hbm, freq_hbm, perm_hbm,
+    kv_hbm, down_hbm, upg_hbm,
     pad, conv, tok, wa, wb, ba, feat, acc, part, rs_in, stage_t, stage_b, seq_in,
     pb, quad_a, red_z_a, red_mid_a, red_y_a, red_bias_a, mf_a,
     quad_b, red_z_b, red_mid_b, red_y_b, red_bias_b, mf_b, ext, grad,
-    ein, e_core, e_mid, e_in1, e_in2, e_all, pt_ref, gb_ref, up_ref, taps_ref, cos_ref, sin_ref, own_b1,
+    ein, e_core, e_mid, e_in1, e_in2, e_all, pt_ref, gb_ref, gb_in, up_ref, taps_ref, cos_ref, sin_ref, own_b1,
+    kv_ref, down_ref, upg_ref, x_ref, depth_ref, dbias_ref, lgain_ref, lshift_ref, b1_ref, rbias_ref, scale_ref, proj_ref, pbias_ref, ngain_ref, kvw_ref, kvb_ref, downw_ref, upw_ref, cot_ref, freq_ref, perm_ref,
     send, recv, lsem,
 ):
+    ids = [0, 0]
+    loads = {}
+
+    def load(name, source, target):
+        loads[name] = pltpu.make_async_copy(source, target, lsem.at[ids[1]])
+        ids[1] += 1
+        loads[name].start()
+
+    load("proj", proj_hbm, proj_ref)
+    load("pbias", pbias_hbm, pbias_ref)
+    load("ngain", ngain_hbm, ngain_ref)
+    load("kvw", kvw_hbm, kvw_ref)
+    load("downw", downw_hbm, downw_ref)
+    load("b1", b1_hbm, b1_ref)
+    load("x", x_hbm, x_ref)
+    load("depth", depth_hbm, depth_ref)
+    load("dbias", dbias_hbm, dbias_ref)
+    load("lgain", lgain_hbm, lgain_ref)
+    load("lshift", lshift_hbm, lshift_ref)
+    load("rbias", rbias_hbm, rbias_ref)
+    load("scale", scale_hbm, scale_ref)
+    load("kvb", kvb_hbm, kvb_ref)
+    load("upw", upw_hbm, upw_ref)
+    load("cot", cot_hbm, cot_ref)
+    load("freq", freq_hbm, freq_ref)
+    load("perm", perm_hbm, perm_ref)
     row = lax.axis_index("row")
     col = lax.axis_index("col")
     x = row // 2
@@ -61,7 +86,6 @@
         xx, yy, zz, kk = (x + dx + 4) % 4, (y + dy + 4) % 4, (z + dz + 4) % 4, (core + dk) % 2
         return (xx * 2 + yy // 2, (yy % 2) * 8 + zz * 2 + kk)
 
-    ids = [0]
 
     def push(src, dst, target):
         n = ids[0]
@@ -81,17 +105,14 @@
     other = device(0, 0, 0, 1)
     yflip = 1 - 2 * ylo
 
-    partners = [up_dev, dn_dev, lt_dev, rt_dev]
-    for dx in range(4):
-        for dk in range(2):
-            if (dx, dk) != (0, 0):
-                partners.append(device(dx, 0, 0, dk))
-    for dy, dz in planes:
-        partners.append(device(0, dy, dz, 0))
-    partners.append(device(0, yflip, 0, 1))
+    partners = [up_dev, dn_dev, lt_dev, rt_dev, other]
+    for step in (1, 2, 3):
+        partners += [device(step, 0, 0, 0), device(0, step, 0, 0), device(0, 0, step, 0)]
     barrier = pltpu.get_barrier_semaphore()
     for partner in partners:
         pl.semaphore_signal(barrier, inc=1, device_id=partner, device_id_type=MESH)
+    for name in ("proj", "pbias", "ngain", "kvw", "downw", "b1"):
+        loads.pop(name).wait()
     diagonal = lax.broadcasted_iota(jnp.int32, (64, 64), 0) == lax.broadcasted_iota(jnp.int32, (64, 64), 1)
     gain = jnp.sum(jnp.where(diagonal, ngain_ref[...].astype(F32), 0.0), axis=1, keepdims=True)
     bias = jnp.sum(jnp.where(diagonal, pbias_ref[...].astype(F32), 0.0), axis=1, keepdims=True)
@@ -104,35 +125,36 @@
     gb_ref[0, :, 0:128] = (downw_ref[...].astype(F32) * gain).astype(BF)
     gb_ref[1:8, :, 0:128] = jnp.zeros((7, 64, 128), BF)
     copies0 = [
-        pltpu.make_async_copy(x_ref, pad.at[3:7, 16:48], lsem.at[0]),
-        pltpu.make_async_copy(w1_ref, wa.at[0], lsem.at[1]),
-        pltpu.make_async_copy(w2_ref, wb.at[0], lsem.at[2]),
-        pltpu.make_async_copy(own_b1, ba.at[0], lsem.at[3]),
-        pltpu.make_async_copy(pt_ref, pb.at[0, :, 0:EXT], lsem.at[4]),
-        pltpu.make_async_copy(gb_ref.at[pair], pb.at[0, :, EXT:2048], lsem.at[5]),
+        pltpu.make_async_copy(x_hbm, pad.at[3:7, 16:48], lsem.at[20]),
+        pltpu.make_async_copy(w1_hbm, wa.at[0], lsem.at[21]),
+        pltpu.make_async_copy(w2_hbm, wb.at[0], lsem.at[22]),
+        pltpu.make_async_copy(own_b1, ba.at[0], lsem.at[23]),
+        pltpu.make_async_copy(pt_ref, pb.at[0, :, 0:EXT], lsem.at[24]),
+        pltpu.make_async_copy(gb_ref.at[pair], pb.at[0, :, EXT:2048], lsem.at[25]),
     ]
     for copy in copies0:
         copy.start()
     pl.semaphore_wait(barrier, len(partners))
 
-    h_up = push(x_ref.at[:, 0:16], pad.at[3:7, 48:64], up_dev)
-    h_dn = push(x_ref.at[:, 16:32], pad.at[3:7, 0:16], dn_dev)
-    h_rt = push(x_ref.at[1:4], pad.at[0:3, 16:48], rt_dev)
-    h_lt = push(x_ref.at[0:3], pad.at[7:10, 16:48], lt_dev)
+    h_up = push(x_hbm.at[:, 0:16], pad.at[3:7, 48:64], up_dev)
+    h_dn = push(x_hbm.at[:, 16:32], pad.at[3:7, 0:16], dn_dev)
+    h_rt = push(x_hbm.at[1:4], pad.at[0:3, 16:48], rt_dev)
+    h_lt = push(x_hbm.at[0:3], pad.at[7:10, 16:48], lt_dev)
     gb_copies = []
     pt_copies = []
     for dx in (1, 3, 2):
         pt_copies.append(push(pt_ref, pb.at[2 * dx, :, 0:EXT], device(dx, 0, 0, 0)))
-    for dx in range(4):
-        for dk in range(2):
-            if (dx, dk) != (0, 0):
-                target_pair = ((x + dx) % 4) * 2 + (core + dk) % 2
-                gb_copies.append(
-                    push(gb_ref.at[target_pair], pb.at[2 * dx + dk, :, EXT:2048], device(dx, 0, 0, dk))
-                )
-    fwd_copies = [push(pt_ref, pb.at[1, :, 0:EXT], other)]
+    for dx in (1, 3, 2):
+        target_x = ((x + dx) % 4) * 2
+        target = device(dx, 0, 0, 0)
+        gb_copies.append(push(gb_ref.at[target_x + core], pb.at[2 * dx, :, EXT:2048], target))
+        gb_copies.append(push(gb_ref.at[target_x + 1 - core], gb_in.at[dx - 1], target))
+    fwd_copies = [
+        push(pt_ref, pb.at[1, :, 0:EXT], other),
+        push(gb_ref.at[x * 2 + 1 - core], pb.at[1, :, EXT:2048], other),
+    ]
     w_core = [
-        push(w1_ref, wa.at[1], other), push(w2_ref, wb.at[1], other), push(own_b1, ba.at[1], other),
+        push(w1_hbm, wa.at[1], other), push(w2_hbm, wb.at[1], other), push(own_b1, ba.at[1], other),
     ]
     x_half = x % 2
 
@@ -146,8 +168,8 @@
     for n in range(2):
         rows1, rows2 = w1_rows(x_half, n, 384), w2_rows(x_half, n, 96)
         w_y.append([
-            push(w1_ref.at[rows1], wa.at[2, rows1], device(0, 1, 0, 0)),
-            push(w2_ref.at[rows2], wb.at[2, rows2], device(0, 3, 0, 0)),
+            push(w1_hbm.at[rows1], wa.at[2, rows1], device(0, 1, 0, 0)),
+            push(w2_hbm.at[rows2], wb.at[2, rows2], device(0, 3, 0, 0)),
         ])
     w_y[0].append(push(own_b1, ba.at[2], device(0, 1, 0, 0)))
 
@@ -160,6 +182,8 @@
         w_x.append(push(wa.at[2, rows1], wa.at[2, rows1], device(1, 0, 0, 0)))
         w_x.append(push(wb.at[2, rows2], wb.at[2, rows2], device(3, 0, 0, 0)))
 
+    for name in list(loads):
+        loads.pop(name).wait()
     token = lax.broadcasted_iota(jnp.int32, (128, 128), 0)
     later = token >= 64
     start = jnp.where(later, start_ref[core * 2 + 1], start_ref[core * 2])
@@ -185,7 +209,7 @@
         copy.wait()
     for n in range(3):
         lanes = slice(n * 512, n * 512 + 512)
-        feat[:, lanes] = dot(perm_ref[...], x_ref[:, :, lanes].reshape(128, 512))
+        feat[:, lanes] = dot(perm_ref[0], x_ref[:, :, lanes].reshape(128, 512))
 
     h_up.wait()
     h_dn.wait()
@@ -208,8 +232,9 @@
     for n, dx in enumerate((1, 3, 2)):
         pt_copies[n].wait()
         fwd_copies.append(push(pb.at[2 * dx, :, 0:EXT], pb.at[2 * dx + 1, :, 0:EXT], other))
-    for copy in gb_copies:
-        copy.wait()
+        gb_copies[2 * n].wait()
+        gb_copies[2 * n + 1].wait()
+        fwd_copies.append(push(gb_in.at[dx - 1], pb.at[2 * dx + 1, :, EXT:2048], other))
     for copy in fwd_copies:
         copy.wait()
 
@@ -414,7 +439,7 @@
     lax.fori_loop(0, 8, norm_rows, 0)
     for n in range(3):
         lanes = slice(n * 512, n * 512 + 512)
-        tok[0, :, lanes] = dot(perm_ref[...], part[0, :, :, lanes].reshape(128, 512)).astype(BF)
+        tok[0, :, lanes] = dot(perm_ref[0], part[0, :, :, lanes].reshape(128, 512)).astype(BF)
     t_next = push(tok.at[0], tok.at[1], device(0, 0, 1, 0))
     t_prev = push(tok.at[0], tok.at[2], device(0, 0, 3, 0))
 
@@ -521,7 +546,7 @@
         copy.wait()
     for n in range(3):
         lanes = slice(n * 512, n * 512 + 512)
-        tok[0, :, lanes] = dot(seq_ref[...], seq_in[:, :, lanes].reshape(128, 512)).astype(BF)
+        tok[0, :, lanes] = dot(perm_ref[1], seq_in[:, :, lanes].reshape(128, 512)).astype(BF)
     for b in range(19):
         if b % 13 == 12:
             ext[:, b * 128:b * 128 + 128] = jnp.where(
@@ -628,12 +653,23 @@
                 kv_ref[:, n * 256 + h * 128:n * 256 + h * 128 + 128] = turned.astype(BF)
         else:
             kv_ref[:, lanes] = value.astype(BF)
+    kv_out = pltpu.make_async_copy(kv_ref, kv_hbm, lsem.at[26])
+    kv_out.start()
     joined.wait()
     down = dot(pt_ref[:, 0:CHANNELS], e_all[0:96].reshape(CHANNELS, 128))
     down_ref[...] = (down + bias * total_shift) * gain
     for n in range(16):
         lanes = slice((n % 8) * 128, (n % 8) * 128 + 128)
         upg_ref[n // 8, :, lanes] = e_all[96 + 4 * n:100 + 4 * n].reshape(64, 128).astype(F32)
+    outs = [
+        pltpu.make_async_copy(upg_ref, upg_hbm, lsem.at[27]),
+        pltpu.make_async_copy(down_ref, down_hbm, lsem.at[28]),
+    ]
+    for copy in outs:
+        copy.start()
+    kv_out.wait()
+    for copy in outs:
+        copy.wait()
 
 
 def orders():
@@ -650,7 +686,7 @@
                     for i in range(2):
                         here = (ys * 2 + cs) * 32 + zs * 8 + w * 2 + i
                         seq[i * 64 + ys * 32 + zs * 8 + cs * 4 + w][here] = 1.0
-    return jnp.array(tile, BF), jnp.array(seq, BF)
+    return jnp.array([tile, seq], BF)
 
 
 def local(
@@ -662,8 +698,7 @@
     cells = feature_grid.transpose(2, 0, 1, 3).reshape(4, 32, CHANNELS)
     freq = np.exp(np.arange(HEAD_DIM // 2, dtype=np.float32) * np.float32(-2.0 * math.log(ROPE_THETA) / HEAD_DIM))
     freq = jnp.array(np.concatenate([freq, freq])[None, :], F32)
-    tile_order, seq_order = orders()
-    vmem = pl.BlockSpec(memory_space=pltpu.VMEM)
+    any_space = pl.BlockSpec(memory_space=pl.ANY)
     kv, down, upg = pl.pallas_call(
         kernel,
         out_shape=(
@@ -671,8 +706,8 @@
             jax.ShapeDtypeStruct((64, 128), F32),
             jax.ShapeDtypeStruct((2, 64, 1024), F32),
         ),
-        in_specs=[vmem] * 5 + [pl.BlockSpec(memory_space=pl.ANY)] * 2 + [vmem] * 10 + [pl.BlockSpec(memory_space=pltpu.SMEM)] + [vmem] * 4,
-        out_specs=(vmem, vmem, vmem),
+        in_specs=[any_space] * 17 + [pl.BlockSpec(memory_space=pltpu.SMEM)] + [any_space] * 3,
+        out_specs=(any_space, any_space, any_space),
         scratch_shapes=[
             pltpu.VMEM((10, 64, CHANNELS), BF),
             pltpu.VMEM((4, 32, CHANNELS), F32),
@@ -710,14 +745,36 @@
             pltpu.VMEM((160, 16, 128), BF),
             pltpu.VMEM((64, EXT), BF),
             pltpu.VMEM((8, 64, 384), BF),
+            pltpu.VMEM((3, 64, 384), BF),
             pltpu.VMEM((128, 2048), BF),
             pltpu.VMEM((7, 8, CHANNELS), F32),
             pltpu.VMEM((128, 128), F32),
             pltpu.VMEM((128, 128), F32),
             pltpu.VMEM((1, 384), F32),
+            pltpu.VMEM((128, 2048), BF),
+            pltpu.VMEM((64, 128), F32),
+            pltpu.VMEM((2, 64, 1024), F32),
+            pltpu.VMEM((4, 32, CHANNELS), BF),
+            pltpu.VMEM((7, 7, CHANNELS), BF),
+            pltpu.VMEM((CHANNELS,), F32),
+            pltpu.VMEM((CHANNELS,), F32),
+            pltpu.VMEM((CHANNELS,), F32),
+            pltpu.VMEM((384,), F32),
+            pltpu.VMEM((CHANNELS,), F32),
+            pltpu.VMEM((CHANNELS,), F32),
+            pltpu.VMEM((64, CHANNELS), BF),
+            pltpu.VMEM((1, 64), BF),
+            pltpu.VMEM((1, 64), BF),
+            pltpu.VMEM((64, 2048), BF),
+            pltpu.VMEM((1, 2048), F32),
+            pltpu.VMEM((64, 128), BF),
+            pltpu.VMEM((2, 64, 1024), BF),
+            pltpu.VMEM((128, 2048), BF),
+            pltpu.VMEM((1, 128), F32),
+            pltpu.VMEM((2, 128, 128), BF),
             pltpu.SemaphoreType.DMA((COPIES,)),
             pltpu.SemaphoreType.DMA((COPIES,)),
-            pltpu.SemaphoreType.DMA((6,)),
+            pltpu.SemaphoreType.DMA((32,)),
         ],
         compiler_params=pltpu.CompilerParams(
             collective_id=0, has_side_effects=True, vmem_limit_bytes=62 << 20
@@ -728,7 +785,7 @@
         expansion_weight, reduction_weight, expansion_bias, reduction_bias,
         layer_branch_scale, projector_weight.T, projector_bias[None, :], input_norm_gain[None, :],
         key_value_weight, key_value_bias[None, :], adapter_down_weight, adapter_up_weight,
-        image_start_positions, key_value_cotangent.reshape(128, 2048), freq, tile_order, seq_order,
+        image_start_positions, key_value_cotangent.reshape(128, 2048), freq, orders(),
     )
     return kv.reshape(2, 64, 2048), down, upg
 

time: 134 us -> 132 us (0.985)
  Pallas kernels: 127 us -> 125 us
    pallas_call x1, Pallas kernels: 127 us -> 125 us  [local(): pl.pallas_call(kernel, out_shape=(jax.ShapeDtypeStruct((128, 2048), BF),...]
where the time goes in v6:
time: 132 us
  Pallas kernels  125 us (95%)
  local copies, waits for them, and re-layouts  5.92 us (4%)
    pallas_call x1, Pallas kernels, local(): pl.pallas_call(kernel, out_shape=(jax.ShapeDtypeStruct((128, 2048), BF),...  125 us
    unnamed x5, local copies, waits for them, and re-layouts  4.11 us

profile of v6, /device:TPU:1, one launch (start us, length us, event | category | flops | bytes accessed | tf_op | source)
XLA Modules:
  0.0 131.6 jit_solution(12687277408453029744)
XLA Ops:
  0.6 1.8 %copy.25.x_hbm = bf16[4,32,1536]{2,1,0:T(8,128)(2,1)} copy(bf16[4,32,1536]{2,0,1:T(4,128)(2,1)} %bitcast.10) | data formatting | bytes 786432 | tf_op jit(solution)/shard_map/reshape | solution.py:698
  2.4 125.0 %shard_map.220 = (bf16[128,2048]{1,0:T(8,128)(2,1)}, f32[64,128]{1,0:T(8,128)}, f32[2,64,1024]{2,1,0:T(8,128)}) custom-call(bf16[4,32,1536]{2,1,0:T(8,128)(2,1)} %copy.25.x_hbm, bf16[7,7,1536]{2,1,0:T(8,128)(2,1)} %depth_hbm.1, f32[1536]{0:T(1024)} %dbias_hbm.1, f32[1536]{0:T(1024)} %lgain_hbm.1, f32[1536]{0:T(1024)} %lshift_hbm.1, ...), custom_call_target="tpu_custom_call" | custom-call | flops 8000000000 | bytes 30000000 | tf_op jit(solution)/shard_map/pallas_call | solution.py:702
  127.5 0.0 copy-start
  127.5 1.9 %copy.29 = bf16[2,64,2048]{2,1,0:T(8,128)(2,1)} copy(bf16[2,64,2048]{2,1,0:T(8,128)(2,1)} %bitcast.9) | data formatting | bytes 1048576
  129.4 1.4 %copy.30 = f32[64,128]{1,0:T(8,128)} copy(f32[64,128]{1,0:T(8,128)} %get-tuple-element.13) | data formatting | bytes 65536
  130.8 0.0 copy-done
  130.8 0.8 copy.31
Async XLA Ops:
  127.5 3.3 %copy-start = (f32[2,64,1024]{2,1,0:T(8,128)S(1)}, f32[2,64,1024]{2,1,0:T(8,128)}, u32[]{:S(2)}) copy-start(f32[2,64,1024]{2,1,0:T(8,128)} %get-tuple-element.14) | copy-start | bytes 1572868
